TPU v7x, 256 devices: a whole 4x4x8 slice. The times are simulated.
256 devices in a mesh: chan: 128 (over x_lo, z, y, core), freq: 2 (over x_hi).
Axes of the slice: x: 4 (x_hi: 2, x_lo: 2; x = x_hi * 2 + x_lo), y: 4, z: 8, core: 2. Of those that a mesh axis runs over, the one named last changes fastest.
Arguments:
- raw_spectra: float32 [4096, 2, 16, 512], P('chan', None, None, 'freq'), may hold values from -1800 to 1800
- valid_windows: int32 [4096], replicated, may hold values from 1 to 16
Outputs:
- correlations: float32 [4, 4096, 32, 128], P(None, ('chan', 'freq'))
All inputs are finite; a program needn't handle non-finite values.
Results may differ from a plain program's by a relative error of at most 0.0003.
Values sent between devices are 32-bit elements; how exact they have to be, the bound alone decides.
No kernel may reach another device: no remote copies, remote signals or barrier semaphores. Data moves between devices by JAX's collectives and lax.ppermute only.
A program may use at most 192 MiB of HBM per device.

v0:
```python
import math

import jax
import jax.numpy as jnp
from jax import lax
from jax.sharding import PartitionSpec as P

FBAND = 512
NFFT = 8192
K0 = 164
LAGS = 128
ROUNDS = 4


def from_partner(block, axis, bit):
    count = lax.axis_size(axis)
    route = []
    for low in range(count):
        high = low | 1 << bit
        if high != low and high < count:
            route += [(low, high), (high, low)]
    return lax.ppermute(block, axis, route)


def lag_tables(first_bin, bin_count):
    bin_index = first_bin + jnp.arange(bin_count, dtype=jnp.int32)
    lag_index = jnp.arange(LAGS, dtype=jnp.int32) - LAGS // 2
    phase_units = bin_index[:, None] * lag_index[None, :] % NFFT
    angles = phase_units.astype(jnp.float32) * (2.0 * math.pi / NFFT)
    return (jnp.cos(angles), jnp.sin(angles))


def correlate(own_rows, own_counts, far_rows, far_counts, cos_table, sin_table):
    highest = lax.Precision.HIGHEST
    window_index = jnp.arange(own_rows.shape[2], dtype=jnp.int32)
    own_mask = (window_index[None, :] < own_counts[:, None]).astype(jnp.float32)
    far_mask = (window_index[None, :] < far_counts[:, None]).astype(jnp.float32)
    own_masked = own_rows * own_mask[:, None, :, None]
    far_masked = far_rows * far_mask[:, None, :, None]
    real_part = jnp.einsum("awf,bwf->abf", own_masked[:, 0], far_masked[:, 0], precision=highest)
    real_part = real_part + jnp.einsum(
        "awf,bwf->abf", own_masked[:, 1], far_masked[:, 1], precision=highest
    )
    imag_part = jnp.einsum("awf,bwf->abf", own_masked[:, 1], far_masked[:, 0], precision=highest)
    imag_part = imag_part - jnp.einsum(
        "awf,bwf->abf", own_masked[:, 0], far_masked[:, 1], precision=highest
    )
    shared_count = jnp.minimum(own_counts[:, None], far_counts[None, :]).astype(jnp.float32)
    real_part = real_part / shared_count[:, :, None]
    imag_part = imag_part / shared_count[:, :, None]
    lagged = jnp.einsum("abf,fl->abl", real_part, cos_table, precision=highest)
    lagged = lagged - jnp.einsum("abf,fl->abl", imag_part, sin_table, precision=highest)
    return lagged / math.sqrt(FBAND)


def on_device(raw_spectra, valid_windows):
    chan_count = raw_spectra.shape[0]
    band_count = raw_spectra.shape[3]
    freq_size = lax.axis_size("freq")
    chan_index = lax.axis_index("chan")
    freq_index = lax.axis_index("freq")
    total_channels = lax.axis_size("chan") * chan_count
    column_sums = lax.psum(jnp.sum(raw_spectra, axis=0), "chan")
    centred = raw_spectra - (column_sums / total_channels)[None]
    local_energy = jnp.sum(centred[:, 0] * centred[:, 0] + centred[:, 1] * centred[:, 1], axis=-1)
    energy = lax.psum(local_energy, "freq") / FBAND
    whitened = centred / jnp.sqrt(energy + 1e-06)[:, None, :, None]
    half_rows = chan_count // freq_size
    round_order = list(range(ROUNDS))
    cos_table, sin_table = lag_tables(K0 + freq_index * band_count, band_count)
    results = [None] * ROUNDS
    for bit_number in round_order:
        partner = jnp.bitwise_xor(chan_index, 1 << bit_number)
        far_rows = from_partner(whitened, "chan", bit_number)
        far_counts = lax.dynamic_slice_in_dim(valid_windows, partner * chan_count, chan_count)
        mine_counts = lax.dynamic_slice_in_dim(
            valid_windows, chan_index * chan_count, half_rows * lax.axis_size("freq")
        )
        results[bit_number] = lax.psum_scatter(
            correlate(whitened, mine_counts, far_rows, far_counts, cos_table, sin_table),
            "freq",
            scatter_dimension=0,
            tiled=True,
        )
    return jnp.stack(results, axis=0)


def solution(mesh):
    return jax.shard_map(
        on_device,
        mesh=mesh,
        in_specs=(P("chan", None, None, "freq"), P()),
        out_specs=P(None, ("chan", "freq"), None, None),
        check_vma=False,
    )
```

profile of v0, /device:TPU:1, one launch (start us, length us, event | category | flops | bytes accessed | tf_op | source)
XLA Modules:
  0.0 907.2 jit_solution(1084424534169942976)
XLA Ops:
  6.5 0.9 fusion.84
  7.6 1.4 reduce_sum.18
  8.9 552.0 %psum.14 = f32[2,16,256]{2,1,0:T(8,128)S(1)} all-reduce(f32[2,16,256]{2,1,0:T(8,128)S(1)} %reduce_sum.18), channel_id=1, replica_groups=mesh['chan'=128,'freq'=2] {'chan'}, use_global_device_ids=true, to_apply=%region_1.0 | all-reduce | flops 8192 | bytes 65536 | tf_op jit(solution)/shard_map/psum | solution.py:63
  560.9 1.4 broadcast_subtract_fusion
  562.5 8.9 psum.15
  571.4 1.2 broadcast_multiply_fusion.3
  572.6 8.6 collective-permute-start
  581.3 1.4 copy.4
  582.7 2.7 copy.7
  585.7 3.3 collective-permute-done.1
  589.0 1.4 broadcast_multiply_fusion.2
  590.4 2.6 copy.11
  593.0 10.2 %fusion.89 = f32[256,32,32]{2,1,0:T(8,128)} fusion(f32[32,16,256]{0,1,2:T(8,128)} %copy.11, f32[32,16,256]{0,1,2:T(8,128)S(1)} %copy.4), kind=kOutput, calls=%fused_computation.131 | convolution fusion | flops 50331648 | bytes 2097152 | tf_op jit(solution)/shard_map/awf,bwf->abf/dot_general | solution.py:40
  603.2 8.7 fusion.91
  611.9 2.6 copy.13
  614.5 10.3 %fusion.90 = f32[256,32,32]{2,1,0:T(8,128)} fusion(f32[32,16,256]{0,1,2:T(8,128)} %copy.13, f32[32,16,256]{0,1,2:T(8,128)} %copy.7), kind=kOutput, calls=%fused_computation.132 | convolution fusion | flops 50331648 | bytes 2097152 | tf_op jit(solution)/shard_map/awf,bwf->abf/dot_general | solution.py:41
  624.8 9.1 %fusion.92 = f32[256,32,32]{2,1,0:T(8,128)} fusion(f32[32,16,256]{0,1,2:T(8,128)S(1)} %copy-done.5, f32[32,16,256]{0,1,2:T(8,128)S(1)} %copy.4), kind=kOutput, calls=%fused_computation.134 | convolution fusion | flops 50331648 | bytes 2097152 | tf_op jit(solution)/shard_map/awf,bwf->abf/dot_general | solution.py:45
  633.9 1.4 broadcast_multiply_fusion.4
  635.4 2.6 copy.6
  638.0 10.3 %fusion.86 = f32[256,32,32]{2,1,0:T(8,128)} fusion(f32[32,16,256]{0,1,2:T(8,128)} %copy.6, f32[32,16,256]{0,1,2:T(8,128)} %copy.7), kind=kOutput, calls=%fused_computation.128 | convolution fusion | flops 50331648 | bytes 2097152 | tf_op jit(solution)/shard_map/awf,bwf->abf/dot_general | solution.py:41
  648.3 8.7 fusion.88
  657.0 4.9 copy.12
  661.8 4.7 copy.14
  666.6 4.7 copy.15
  671.2 4.7 copy.16
  676.0 3.2 fusion.6
  679.2 2.3 fusion.1
  681.6 2.7 copy.3
  684.3 10.2 %fusion.85 = f32[256,32,32]{2,1,0:T(8,128)} fusion(f32[32,16,256]{0,1,2:T(8,128)} %copy.3, f32[32,16,256]{0,1,2:T(8,128)S(1)} %copy.4), kind=kOutput, calls=%fused_computation.127 | convolution fusion | flops 50331648 | bytes 2097152 | tf_op jit(solution)/shard_map/awf,bwf->abf/dot_general | solution.py:40
  694.4 8.7 fusion.87
  703.1 1.4 broadcast_multiply_fusion.1
  704.6 2.6 copy.17
  707.2 10.2 %fusion.93 = f32[256,32,32]{2,1,0:T(8,128)} fusion(f32[32,16,256]{0,1,2:T(8,128)} %copy.17, f32[32,16,256]{0,1,2:T(8,128)S(1)} %copy.4), kind=kOutput, calls=%fused_computation.135 | convolution fusion | flops 50331648 | bytes 2097152 | tf_op jit(solution)/shard_map/awf,bwf->abf/dot_general | solution.py:40
  717.4 2.6 copy.19
  720.0 10.1 %fusion.94 = f32[256,32,32]{2,1,0:T(8,128)} fusion(f32[32,16,256]{0,1,2:T(8,128)} %copy.19, f32[32,16,256]{0,1,2:T(8,128)} %copy.7), kind=kOutput, calls=%fused_computation.136 | convolution fusion | flops 50331648 | bytes 2097152 | tf_op jit(solution)/shard_map/awf,bwf->abf/dot_general | solution.py:41
  730.1 4.7 copy.5
  734.8 4.7 copy.8
  739.5 4.7 copy.10
  744.2 4.7 copy.9
  748.9 4.7 copy.18
  753.6 4.8 copy.20
  758.4 10.3 %fusion.95 = f32[256,32,32]{2,1,0:T(8,128)} fusion(f32[32,16,256]{0,1,2:T(8,128)} %copy.17, f32[32,16,256]{0,1,2:T(8,128)} %copy.7), kind=kOutput, calls=%fused_computation.137 | convolution fusion | flops 50331648 | bytes 2097152 | tf_op jit(solution)/shard_map/awf,bwf->abf/dot_general | solution.py:44
  768.6 4.7 copy.21
  773.3 9.8 %fusion.96 = f32[256,32,32]{2,1,0:T(8,128)} fusion(f32[32,16,256]{0,1,2:T(8,128)} %copy.19, f32[32,16,256]{0,1,2:T(8,128)S(1)} %copy.4), kind=kOutput, calls=%fused_computation.138 | convolution fusion | flops 50331648 | bytes 2097152 | tf_op jit(solution)/shard_map/awf,bwf->abf/dot_general | solution.py:45
  783.1 4.9 copy.22
  788.0 1.4 broadcast_multiply_fusion
  789.5 2.6 copy.25
  792.1 2.6 copy.23
  794.7 3.2 fusion.7
  798.0 2.3 fusion
  800.4 2.9 fusion.5
  803.3 2.3 fusion.2
  805.7 10.2 %fusion.97 = f32[256,32,32]{2,1,0:T(8,128)} fusion(f32[32,16,256]{0,1,2:T(8,128)} %copy.23, f32[32,16,256]{0,1,2:T(8,128)S(1)} %copy.4), kind=kOutput, calls=%fused_computation.139 | convolution fusion | flops 50331648 | bytes 2097152 | tf_op jit(solution)/shard_map/awf,bwf->abf/dot_general | solution.py:40
  815.9 8.7 fusion.99
  824.6 10.6 %fusion.98 = f32[256,32,32]{2,1,0:T(8,128)} fusion(f32[32,16,256]{0,1,2:T(8,128)} %copy.25, f32[32,16,256]{0,1,2:T(8,128)} %copy.7), kind=kOutput, calls=%fused_computation.140 | convolution fusion | flops 50331648 | bytes 2097152 | tf_op jit(solution)/shard_map/awf,bwf->abf/dot_general | solution.py:41
  835.2 4.8 copy.26
  840.0 4.7 copy.24
  844.7 4.2 copy.27
  848.9 9.8 %fusion.100 = f32[256,32,32]{2,1,0:T(8,128)} fusion(f32[32,16,256]{0,1,2:T(8,128)} %copy.25, f32[32,16,256]{0,1,2:T(8,128)S(1)} %copy.4), kind=kOutput, calls=%fused_computation.142 | convolution fusion | flops 50331648 | bytes 2097152 | tf_op jit(solution)/shard_map/awf,bwf->abf/dot_general | solution.py:45
  858.7 5.0 copy.28
  863.8 1.5 fusion.4
  865.3 2.3 fusion.3
  867.8 30.4 %reduce-scatter.11.cloned.1.call-done = f32[16,32,128]{2,1,0:T(8,128)} async-done(((f32[32,32,128]{2,1,0:T(8,128)}), f32[16,32,128]{2,1,0:T(8,128)}) %reduce-scatter.11.cloned.1.call-update) | async-done | bytes 262160 | tf_op jit(solution)/shard_map/reduce_scatter | solution.py:79
  898.2 2.2 pad_maximum_fusion
  (71 shorter events, 1.3 us)
Async XLA Ops:
  6.5 861.2 %reduce-scatter.7.cloned.1.call-start = ((), (), s32[]{:S(2)}) async-start(), calls=%async_computation.5 | async-start | bytes 786432 | tf_op jit(solution)/shard_map/reduce_scatter | solution.py:79
  7.6 563.8 %copy-start.8 = (f32[32,2,16,256]{3,2,1,0:T(8,128)S(1)}, f32[32,2,16,256]{3,2,1,0:T(8,128)}, u32[]{:S(2)}) copy-start(f32[32,2,16,256]{3,2,1,0:T(8,128)} %param.2) | copy-start | bytes 3145732
  572.6 16.4 %collective-permute-start.1 = (f32[32,2,16,256]{3,2,1,0:T(8,128)}, f32[32,2,16,256]{3,2,1,0:T(8,128)}, u32[]{:S(2)}, u32[]{:S(2)}) collective-permute-start(f32[32,2,16,256]{3,2,1,0:T(8,128)} %get-tuple-element.6), channel_id=1, source_target_pairs={{0,4},{4,0},{2,6},{6,2},{8,12},{12,8},{10,14},{14,10},{16,20},{20,... | collective-permute-start | bytes 3145736 | tf_op jit(solution)/shard_map/ppermute | solution.py:22
  572.6 61.4 %collective-permute-start = (f32[32,2,16,256]{3,2,1,0:T(8,128)}, f32[32,2,16,256]{3,2,1,0:T(8,128)}, u32[]{:S(2)}, u32[]{:S(2)}) collective-permute-start(f32[32,2,16,256]{3,2,1,0:T(8,128)} %get-tuple-element.6), channel_id=1, source_target_pairs={{0,2},{2,0},{4,6},{6,4},{8,10},{10,8},{12,14},{14,12},{16,18},{18,... | collective-permute-start | bytes 3145736 | tf_op jit(solution)/shard_map/ppermute | solution.py:22
  581.1 122.0 %collective-permute-start.2 = (f32[32,2,16,256]{3,2,1,0:T(8,128)}, f32[32,2,16,256]{3,2,1,0:T(8,128)}, u32[]{:S(2)}, u32[]{:S(2)}) collective-permute-start(f32[32,2,16,256]{3,2,1,0:T(8,128)} %get-tuple-element.6), channel_id=1, source_target_pairs={{0,8},{8,0},{2,10},{10,2},{4,12},{12,4},{6,14},{14,6},{16,24},{24,... | collective-permute-start | bytes 3145736 | tf_op jit(solution)/shard_map/ppermute | solution.py:22
  581.1 206.9 %collective-permute-start.3 = (f32[32,2,16,256]{3,2,1,0:T(8,128)}, f32[32,2,16,256]{3,2,1,0:T(8,128)}, u32[]{:S(2)}, u32[]{:S(2)}) collective-permute-start(f32[32,2,16,256]{3,2,1,0:T(8,128)} %get-tuple-element.6), channel_id=1, source_target_pairs={{0,16},{16,0},{2,18},{18,2},{4,20},{20,4},{6,22},{22,6},{8,24},{24... | collective-permute-start | bytes 3145736 | tf_op jit(solution)/shard_map/ppermute | solution.py:22
  593.0 10.2 %copy-start = (f32[32,16,256]{0,1,2:T(8,128)S(1)}, f32[32,16,256]{0,1,2:T(8,128)}, u32[]{:S(2)}) copy-start(f32[32,16,256]{0,1,2:T(8,128)} %copy.7) | copy-start | bytes 1572868
  593.0 10.2 %copy-start.4 = (f32[32,16,256]{0,1,2:T(8,128)S(1)}, f32[32,16,256]{0,1,2:T(8,128)}, u32[]{:S(2)}) copy-start(f32[32,16,256]{0,1,2:T(8,128)} %copy.11) | copy-start | bytes 1572868
  614.5 10.3 %copy-start.5 = (f32[32,16,256]{0,1,2:T(8,128)S(1)}, f32[32,16,256]{0,1,2:T(8,128)}, u32[]{:S(2)}) copy-start(f32[32,16,256]{0,1,2:T(8,128)} %copy.13) | copy-start | bytes 1572868
  638.0 10.3 %copy-start.6 = (f32[32,16,256]{0,1,2:T(8,128)S(1)}, f32[32,16,256]{0,1,2:T(8,128)}, u32[]{:S(2)}) copy-start(f32[32,16,256]{0,1,2:T(8,128)} %copy.6) | copy-start | bytes 1572868
  676.0 3.2 copy-start.17
  676.0 3.2 copy-start.18
  681.5 186.2 %reduce-scatter.5.cloned.1.call-start = ((), (), s32[]{:S(2)}) async-start(), calls=%async_computation.4 | async-start | bytes 786432 | tf_op jit(solution)/shard_map/reduce_scatter | solution.py:79
  684.3 10.2 %copy-start.1 = (f32[32,16,256]{0,1,2:T(8,128)S(1)}, f32[32,16,256]{0,1,2:T(8,128)}, u32[]{:S(2)}) copy-start(f32[32,16,256]{0,1,2:T(8,128)} %copy.7) | copy-start | bytes 1572868
  684.3 10.2 %copy-start.7 = (f32[32,16,256]{0,1,2:T(8,128)S(1)}, f32[32,16,256]{0,1,2:T(8,128)}, u32[]{:S(2)}) copy-start(f32[32,16,256]{0,1,2:T(8,128)} %copy.3) | copy-start | bytes 1572868
  794.7 3.2 copy-start.12
  794.7 3.2 copy-start.13
  798.0 2.4 copy-start.9
  800.3 67.4 %reduce-scatter.9.cloned.1.call-start = ((), (), s32[]{:S(2)}) async-start(), calls=%async_computation.6 | async-start | bytes 786432 | tf_op jit(solution)/shard_map/reduce_scatter | solution.py:79
  800.4 2.9 copy-start.10
  800.4 2.9 copy-start.11
  805.7 10.2 %copy-start.2 = (f32[32,16,256]{0,1,2:T(8,128)S(1)}, f32[32,16,256]{0,1,2:T(8,128)}, u32[]{:S(2)}) copy-start(f32[32,16,256]{0,1,2:T(8,128)} %copy.7) | copy-start | bytes 1572868
  805.7 10.2 %copy-start.3 = (f32[32,16,256]{0,1,2:T(8,128)S(1)}, f32[32,16,256]{0,1,2:T(8,128)}, u32[]{:S(2)}) copy-start(f32[32,16,256]{0,1,2:T(8,128)} %copy.23) | copy-start | bytes 1572868
  824.6 73.6 %reduce-scatter.11.cloned.1.call-start = ((), (), s32[]{:S(2)}) async-start(), calls=%async_computation.7 | async-start | bytes 786432 | tf_op jit(solution)/shard_map/reduce_scatter | solution.py:79
  858.7 5.0 copy-start.14
  858.7 5.0 copy-start.15
  863.8 1.5 copy-start.16
Sparse Core Ops, SparseCore 0:
  681.7 30.5 reduce-scatter.6
  800.5 30.4 reduce-scatter.4
  833.5 21.6 reduce-scatter.8
  867.8 30.3 reduce-scatter.10
where the time goes:
time: 913 us; the launch traced here: 907 us
  blocking collectives  561 us (61%)
  matrix products  176 us (19%)
  local copies, waits for them, and re-layouts  102 us (11%)
  waiting for transfers between devices  33.8 us (4%)
  between operations  13.7 us (2%)
  other arithmetic  12.2 us (1%)
    psum x1, blocking collectives, on_device(): column_sums = lax.psum(jnp.sum(raw_spectra, axis=0), 'chan')  552 us
    dot_general x4, matrix products, correlate(): jnp.einsum('awf,bwf->abf', own_masked[:, 1], far_masked[:, 1], precision=...  41.3 us
    dot_general x4, matrix products, correlate(): jnp.einsum('awf,bwf->abf', own_masked[:, 0], far_masked[:, 0], precision=...  40.7 us
    dot_general x4, matrix products, correlate(): jnp.einsum('awf,bwf->abf', own_masked[:, 0], far_masked[:, 1], precision=...  37.4 us
    dot_general x4, matrix products, correlate(): jnp.einsum('awf,bwf->abf', own_masked[:, 1], far_masked[:, 0], precision=...  36.3 us
    reduce_scatter x4, waiting for transfers between devices, on_device(): lax.psum_scatter(correlate(whitened, mine_counts, far_rows, far_counts, c...  30.5 us
    dot_general x4, local copies, waits for them, and re-layouts, correlate(): jnp.einsum('awf,bwf->abf', own_masked[:, 0], far_masked[:, 1], precision=...  19.3 us
    dot_general x4, local copies, waits for them, and re-layouts, correlate(): jnp.einsum('awf,bwf->abf', own_masked[:, 0], far_masked[:, 0], precision=...  19 us
  transfers between devices with their start and end apart: 8, of which 2 were waited for; matrix products, arithmetic and copies ran while one was open for 31% of the time, Pallas kernels for 0%

commit v1 on v0

v1 whole, which is shorter than its diff:
```python
import functools
import math

import jax
import jax.numpy as jnp
from jax import lax
from jax.experimental import pallas as pl
from jax.experimental.pallas import tpu as pltpu
from jax.sharding import PartitionSpec as P

F32 = jnp.float32
BF16 = jnp.bfloat16
FBAND = 512
NFFT = 8192
K0 = 164
LAGS = 128
ROUNDS = 4
WINDOWS = 16
A_TILE = 4
LANE = 128


def parity_of(index):
    return (index ^ (index >> 1) ^ (index >> 2) ^ (index >> 3)) & 1


def owner_round(parity, freq):
    return parity + 2 * freq


def edge_route(chan_count, flip):
    route = []
    for chan in range(chan_count):
        for freq in range(2):
            far = chan ^ (1 << owner_round(parity_of(chan), freq))
            route.append((chan * 2 + freq, far * 2 + (freq ^ flip)))
    return route


def xor_permute(block, bit, chan_count):
    return lax.ppermute(block, "chan", [(i, i ^ bit) for i in range(chan_count)])


def swap_freq(block):
    return lax.ppermute(block, "freq", [(0, 1), (1, 0)])


def lag_tables(first_bin, bin_count):
    bin_index = first_bin + jnp.arange(bin_count, dtype=jnp.int32)
    lag_index = jnp.arange(LAGS, dtype=jnp.int32) - LAGS // 2
    phase_units = bin_index[:, None] * lag_index[None, :] % NFFT
    angles = phase_units.astype(F32) * (2.0 * math.pi / NFFT)
    return (jnp.cos(angles), jnp.sin(angles))


def split_table(table):
    high = lax.reduce_precision(table, 8, 7)
    return jnp.concatenate([high.astype(BF16), (table - high).astype(BF16)], axis=1)


def edge_body(
    place, own0, own1_re, own1_im, far0, far1_re, far1_im, mean0, mean1, own_n, far_n, cos_t, sin_t,
    keep_ref, other_ref, far_ref, a_rows, b_rows, g_high, g_low,
):
    half = own0.shape[3]
    chans = own0.shape[2]
    hrows = chans // 2
    b0 = pl.multiple_of(place[0], hrows)
    a_keep = place[1]

    def whiten(low, high, rows, counts, put):
        for w in range(WINDOWS):
            re0 = low[0, w, rows, :] - mean0[0, pl.ds(w, 1), :]
            im0 = low[1, w, rows, :] - mean0[1, pl.ds(w, 1), :]
            re1 = high[0][w, rows, :] - mean1[0, pl.ds(w, 1), :]
            im1 = high[1][w, rows, :] - mean1[1, pl.ds(w, 1), :]
            energy = jnp.sum(re0 * re0 + im0 * im0 + re1 * re1 + im1 * im1, axis=1, keepdims=True)
            scale = lax.rsqrt(energy * (1.0 / FBAND) + 1e-06)
            scale = jnp.where(counts > float(w), scale, 0.0)
            put(w, re0 * scale, im0 * scale, re1 * scale, im1 * scale)

    def put_own(w, re0, im0, re1, im1):
        for k, (v0, v1) in enumerate(((re0, re1), (im0, im1), (re0 + im0, re1 + im1))):
            for c, v in enumerate((v0[:, :LANE], v0[:, LANE:], v1[:, :LANE], v1[:, LANE:])):
                a_rows[c, pl.ds(k * WINDOWS + w, chans, stride=3 * WINDOWS), :] = v

    def put_far(w, re0, im0, re1, im1):
        for k, (v0, v1) in enumerate(((re0 + im0, re1 + im1), (im0 - re0, im1 - re1), (re0, re1))):
            b_rows[k, w, :, :half] = v0
            b_rows[k, w, :, half:] = v1

    whiten(own0, (own1_re, own1_im), slice(0, chans), own_n[:, 0:1], put_own)
    whiten(far0, (far1_re, far1_im), pl.ds(b0, hrows), far_n[pl.ds(b0, hrows), 0:1], put_far)

    def products(t, carry):
        a0 = t * A_TILE
        for c in range(2 * half // LANE):
            lanes = slice(c * LANE, (c + 1) * LANE)
            sums = [[None] * 3 for _ in range(A_TILE)]
            for w in range(WINDOWS):
                far = [b_rows[k, w, :, lanes] for k in range(3)]
                for j in range(A_TILE):
                    for k in range(3):
                        own = a_rows[c, pl.ds((a0 + j) * (3 * WINDOWS) + k * WINDOWS + w, 1), :]
                        term = own * far[k]
                        sums[j][k] = term if w == 0 else sums[j][k] + term
            for j in range(A_TILE):
                s_im, s_re, s_both = sums[j]
                rows = pl.ds(pl.multiple_of((a0 + j) * hrows, hrows), hrows)
                for part, value in enumerate((s_both + s_re, s_both - s_im)):
                    high = value.astype(BF16)
                    at = slice(part * 2 * half + c * LANE, part * 2 * half + (c + 1) * LANE)
                    g_high[rows, at] = high
                    g_low[rows, at] = (value - high.astype(F32)).astype(BF16)
        return carry

    lax.fori_loop(0, chans // A_TILE, products, 0)
    far_counts = far_n[pl.ds(b0, hrows), :]
    group = 8

    def lagged(t, carry):
        size = group * hrows
        rows = pl.ds(pl.multiple_of(t * size, size), size)

        def project(part, table):
            at = slice(part * 2 * half, (part + 1) * 2 * half)
            both = jnp.dot(g_high[rows, at], table[...], preferred_element_type=F32)
            low = jnp.dot(g_low[rows, at], table[:, :LAGS], preferred_element_type=F32)
            return both[:, :LAGS] + both[:, LAGS:] + low

        real = project(0, cos_t)
        imag = project(1, sin_t)
        forward = real - imag
        backward = real + imag
        for j in range(group):
            a = t * group + j
            shared = jnp.minimum(far_counts, own_n[pl.ds(a, 1), :])
            scale = (1.0 / math.sqrt(FBAND)) / shared
            at = slice(j * hrows, (j + 1) * hrows)
            far_ref[:, a, :] = backward[at] * scale
            value = forward[at] * scale
            mine = (a >= a_keep) & (a < a_keep + hrows)

            @pl.when(mine)
            def _():
                keep_ref[a - a_keep] = value

            @pl.when(jnp.logical_not(mine))
            def _():
                other_ref[a - (hrows - a_keep)] = value

        return carry

    lax.fori_loop(0, chans // group, lagged, 0)


def edge(place, own0, own1_re, own1_im, far0, far1_re, far1_im, mean0, mean1, own_n, far_n, cos_t, sin_t):
    chans = own0.shape[2]
    band = 2 * own0.shape[3]
    hrows = chans // 2
    vmem = pl.BlockSpec(memory_space=pltpu.VMEM)
    return pl.pallas_call(
        edge_body,
        out_shape=(
            jax.ShapeDtypeStruct((hrows, hrows, LAGS), F32),
            jax.ShapeDtypeStruct((hrows, hrows, LAGS), F32),
            jax.ShapeDtypeStruct((hrows, chans, LAGS), F32),
        ),
        in_specs=[pl.BlockSpec(memory_space=pltpu.SMEM)] + [vmem] * 12,
        out_specs=(vmem, vmem, vmem),
        scratch_shapes=[
            pltpu.VMEM((band // LANE, chans * 3 * WINDOWS, LANE), F32),
            pltpu.VMEM((3, WINDOWS, hrows, band), F32),
            pltpu.VMEM((chans * hrows, 2 * band), BF16),
            pltpu.VMEM((chans * hrows, 2 * band), BF16),
        ],
        compiler_params=pltpu.CompilerParams(vmem_limit_bytes=40 * 1024 * 1024),
        cost_estimate=pl.CostEstimate(flops=800_000_000, bytes_accessed=5_000_000, transcendentals=0),
        name="edge",
    )(place, own0, own1_re, own1_im, far0, far1_re, far1_im, mean0, mean1, own_n, far_n, cos_t, sin_t)


def on_device(raw_spectra, valid_windows):
    chans, _, _, half = raw_spectra.shape
    hrows = chans // 2
    size = lax.axis_size("chan")
    chan_index = lax.axis_index("chan")
    freq_index = lax.axis_index("freq")
    barrier = lax.optimization_barrier

    def to_partner(block, flip):
        return lax.ppermute(block, ("chan", "freq"), edge_route(size, flip))

    def from_partner(block):
        route = [(low, high) for high, low in edge_route(size, 0)]
        return lax.ppermute(block, ("chan", "freq"), route)

    sums = jnp.sum(raw_spectra, axis=0)
    top = size // 2
    sums = sums + xor_permute(sums, top, size)
    block = jnp.transpose(raw_spectra, (1, 2, 0, 3))
    block, sums = barrier((block, sums))
    far_mine = from_partner(block)
    early = swap_freq(block[0])
    late = swap_freq(block[1])
    for bit in (1, 8, 16, 32):
        sums = barrier(sums + xor_permute(sums, bit, size))
    early, sums = barrier((early, sums))
    far_early = from_partner(early)
    for bit in (4, 2):
        sums = barrier(sums + xor_permute(sums, bit, size))
    mean = sums / (size * chans)
    mean_other = swap_freq(mean)
    late, mean_other = barrier((late, mean_other))
    far_late = from_partner(late)

    parity = parity_of(chan_index)
    my_round = owner_round(parity, freq_index)
    partner = chan_index ^ (1 << my_round)

    def counts(index):
        part = lax.dynamic_slice_in_dim(valid_windows, index * chans, chans)
        return jnp.broadcast_to(part.astype(F32)[:, None], (chans, LANE))

    mine_t = lag_tables(K0 + freq_index * half, half)
    other_t = lag_tables(K0 + (1 - freq_index) * half, half)
    cos_t, sin_t = [split_table(jnp.concatenate(pair, axis=0)) for pair in zip(mine_t, other_t)]

    def work(b0):
        place = jnp.stack([b0, freq_index * hrows]).astype(jnp.int32)
        return edge(
            place, block, early, late, far_mine, far_early, far_late,
            mean, mean_other, counts(chan_index), counts(partner), cos_t, sin_t,
        )

    b_first = (1 - freq_index) * hrows
    b_second = freq_index * hrows
    keep1, other1, far1 = work(b_first)
    far1 = to_partner(far1, 1)
    other1 = swap_freq(other1)
    keep2, other2, far2 = work(b_second)
    far2 = to_partner(far2, 0)
    other2 = swap_freq(other2)

    out = jnp.zeros((ROUNDS, hrows, chans, LAGS), F32)

    def place_at(out, part, at_round, at_row):
        zero = jnp.int32(0)
        return lax.dynamic_update_slice(out, part[None], (at_round, zero, at_row, zero))

    other_round = owner_round(parity, 1 - freq_index)
    out = place_at(out, keep1, my_round, b_first)
    out = place_at(out, keep2, my_round, b_second)
    zero = jnp.int32(0)
    out = place_at(out, far1, owner_round(1 - parity, 1 - freq_index), zero)
    out = place_at(out, other1, other_round, b_second)
    out = place_at(out, other2, other_round, b_first)
    out = place_at(out, far2, owner_round(1 - parity, freq_index), zero)
    return out


def solution(mesh):
    return jax.shard_map(
        on_device,
        mesh=mesh,
        in_specs=(P("chan", None, None, "freq"), P()),
        out_specs=P(None, ("chan", "freq"), None, None),
        check_vma=False,
    )
```

time: 913 us -> 92.7 us (0.10)
  the two profiles are of different devices: /device:TPU:1 before, /device:TPU:6 now
where the time goes in v1:
time: 92.7 us; the launch traced here: 92.5 us
  starting transfers between devices  34.5 us (37%)
  waiting for transfers between devices  32.8 us (35%)
  Pallas kernels  17 us (18%)
  other arithmetic  5.38 us (6%)
  local copies, waits for them, and re-layouts  2.59 us (3%)
    pallas_call x2, Pallas kernels, edge(): pl.pallas_call(edge_body, out_shape=(jax.ShapeDtypeStruct((hrows, hrows,...  17 us
    ppermute x7, starting transfers between devices, xor_permute(): lax.ppermute(block, 'chan', [(i, i ^ bit) for i in range(chan_count)])  17 us
    ppermute x3, waiting for transfers between devices, from_partner(): return lax.ppermute(block, ('chan', 'freq'), route)  13.9 us
    ppermute x7, waiting for transfers between devices, xor_permute(): lax.ppermute(block, 'chan', [(i, i ^ bit) for i in range(chan_count)])  11 us
    ppermute x5, starting transfers between devices, swap_freq(): return lax.ppermute(block, 'freq', [(0, 1), (1, 0)])  9.99 us
    ppermute x5, waiting for transfers between devices, swap_freq(): return lax.ppermute(block, 'freq', [(0, 1), (1, 0)])  4.5 us
    ppermute x3, starting transfers between devices, from_partner(): return lax.ppermute(block, ('chan', 'freq'), route)  4.28 us
    ppermute x2, waiting for transfers between devices, to_partner(): return lax.ppermute(block, ('chan', 'freq'), edge_route(size, flip))  3.4 us
  transfers between devices with their start and end apart: 17, of which 13 were waited for; matrix products, arithmetic and copies ran while one was open for 5% of the time, Pallas kernels for 9%

profile of v1, /device:TPU:6, one launch (start us, length us, event | category | flops | bytes accessed | tf_op | source)
XLA Modules:
  0.0 92.5 jit_solution(8960391838543784794)
XLA Ops:
  0.0 0.0 copy-start
  0.0 1.4 %reduce_sum.9 = f32[2,16,256]{2,1,0:T(8,128)S(1)} reduce(f32[32,2,16,256]{3,2,1,0:T(8,128)} %param.2, f32[]{:T(128)} %constant.18.clone.1), dimensions={0}, to_apply=%region_0.0 | reduce | flops 253952 | bytes 1081348 | tf_op jit(solution)/shard_map/reduce_sum | solution.py:198
  1.4 0.9 collective-permute-start
  2.3 0.0 copy-done
  2.3 0.6 copy.5
  2.9 2.5 %collective-permute-done = f32[2,16,256]{2,1,0:T(8,128)S(1)} collective-permute-done((f32[2,16,256]{2,1,0:T(8,128)S(1)}, f32[2,16,256]{2,1,0:T(8,128)S(1)}, u32[]{:S(2)}, u32[]{:S(2)}) %collective-permute-start) | collective-permute-done | bytes 32800 | tf_op jit(solution)/shard_map/ppermute | solution.py:41
  5.4 0.9 slice_bitcast_fusion
  6.3 1.7 %collective-permute-start.1 = (f32[16,32,256]{2,1,0:T(8,128)S(1)}, f32[16,32,256]{2,1,0:T(8,128)S(1)}, u32[]{:S(2)}, u32[]{:S(2)}) collective-permute-start(f32[16,32,256]{2,1,0:T(8,128)S(1)} %get-tuple-element.30), channel_id=1, source_target_pairs={{0,1},{1,0},{2,3},{3,2},{4,5},{5,4},{6,7},{7,6},{8,9},{9,8},{10,11... | collective-permute-start | bytes 1572872 | tf_op jit(solution)/shard_map/ppermute | solution.py:45
  8.0 0.0 collective-permute-start.2
  8.0 1.2 %collective-permute-done.2 = f32[2,16,256]{2,1,0:T(8,128)S(1)} collective-permute-done((f32[2,16,256]{2,1,0:T(8,128)S(1)}, f32[2,16,256]{2,1,0:T(8,128)S(1)}, u32[]{:S(2)}, u32[]{:S(2)}) %collective-permute-start.2) | collective-permute-done | bytes 32800 | tf_op jit(solution)/shard_map/ppermute | solution.py:41
  9.2 1.7 %collective-permute-start.3 = (f32[2,16,256]{2,1,0:T(8,128)S(1)}, f32[2,16,256]{2,1,0:T(8,128)S(1)}, u32[]{:S(2)}, u32[]{:S(2)}) collective-permute-start(f32[2,16,256]{2,1,0:T(8,128)S(1)} %add.105), channel_id=1, source_target_pairs={{0,16},{2,18},{4,20},{6,22},{8,24},{10,26},{12,28},{14,30},{16,0},... | collective-permute-start | bytes 98312 | tf_op jit(solution)/shard_map/ppermute | solution.py:41
  10.8 2.2 %collective-permute-done.3 = f32[2,16,256]{2,1,0:T(8,128)S(1)} collective-permute-done((f32[2,16,256]{2,1,0:T(8,128)S(1)}, f32[2,16,256]{2,1,0:T(8,128)S(1)}, u32[]{:S(2)}, u32[]{:S(2)}) %collective-permute-start.3) | collective-permute-done | bytes 32800 | tf_op jit(solution)/shard_map/ppermute | solution.py:41
  13.1 3.0 %collective-permute-start.4 = (f32[2,16,256]{2,1,0:T(8,128)S(1)}, f32[2,16,256]{2,1,0:T(8,128)S(1)}, u32[]{:S(2)}, u32[]{:S(2)}) collective-permute-start(f32[2,16,256]{2,1,0:T(8,128)S(1)} %add.106), channel_id=1, source_target_pairs={{0,32},{2,34},{4,36},{6,38},{8,40},{10,42},{12,44},{14,46},{16,48}... | collective-permute-start | bytes 98312 | tf_op jit(solution)/shard_map/ppermute | solution.py:41
  16.1 2.2 %collective-permute-done.4 = f32[2,16,256]{2,1,0:T(8,128)S(1)} collective-permute-done((f32[2,16,256]{2,1,0:T(8,128)S(1)}, f32[2,16,256]{2,1,0:T(8,128)S(1)}, u32[]{:S(2)}, u32[]{:S(2)}) %collective-permute-start.4) | collective-permute-done | bytes 32800 | tf_op jit(solution)/shard_map/ppermute | solution.py:41
  18.3 6.5 %collective-permute-start.5 = (f32[2,16,256]{2,1,0:T(8,128)S(1)}, f32[2,16,256]{2,1,0:T(8,128)S(1)}, u32[]{:S(2)}, u32[]{:S(2)}) collective-permute-start(f32[2,16,256]{2,1,0:T(8,128)S(1)} %add.107), channel_id=1, source_target_pairs={{0,64},{2,66},{4,68},{6,70},{8,72},{10,74},{12,76},{14,78},{16,80}... | collective-permute-start | bytes 98312 | tf_op jit(solution)/shard_map/ppermute | solution.py:41
  24.9 1.9 %collective-permute-done.5 = f32[2,16,256]{2,1,0:T(8,128)S(1)} collective-permute-done((f32[2,16,256]{2,1,0:T(8,128)S(1)}, f32[2,16,256]{2,1,0:T(8,128)S(1)}, u32[]{:S(2)}, u32[]{:S(2)}) %collective-permute-start.5) | collective-permute-done | bytes 32800 | tf_op jit(solution)/shard_map/ppermute | solution.py:41
  26.8 0.0 collective-permute-done.1.own1_re
  26.8 3.3 %collective-permute-start.7 = (f32[2,16,256]{2,1,0:T(8,128)S(1)}, f32[2,16,256]{2,1,0:T(8,128)S(1)}, u32[]{:S(2)}, u32[]{:S(2)}) collective-permute-start(f32[2,16,256]{2,1,0:T(8,128)S(1)} %add.108), channel_id=1, source_target_pairs={{0,8},{2,10},{4,12},{6,14},{8,0},{10,2},{12,4},{14,6},{16,24},{18,... | collective-permute-start | bytes 98312 | tf_op jit(solution)/shard_map/ppermute | solution.py:41
  30.0 2.1 %collective-permute-start.6 = (f32[16,32,256]{2,1,0:T(8,128)}, f32[16,32,256]{2,1,0:T(8,128)S(1)}, u32[]{:S(2)}, u32[]{:S(2)}) collective-permute-start(f32[16,32,256]{2,1,0:T(8,128)} %get-tuple-element.29), channel_id=1, source_target_pairs={{0,1},{1,0},{2,3},{3,2},{4,5},{5,4},{6,7},{7,6},{8,9},{9,8},{10,11... | collective-permute-start | bytes 1572872 | tf_op jit(solution)/shard_map/ppermute | solution.py:45
  32.2 0.1 collective-permute-done.7
  32.3 1.6 %collective-permute-start.8 = (f32[2,16,256]{2,1,0:T(8,128)S(1)}, f32[2,16,256]{2,1,0:T(8,128)S(1)}, u32[]{:S(2)}, u32[]{:S(2)}) collective-permute-start(f32[2,16,256]{2,1,0:T(8,128)S(1)} %add.109), channel_id=1, source_target_pairs={{0,4},{2,6},{4,0},{6,2},{8,12},{10,14},{12,8},{14,10},{16,20},{18,... | collective-permute-start | bytes 98312 | tf_op jit(solution)/shard_map/ppermute | solution.py:41
  33.9 1.5 %collective-permute-start.10 = (f32[2,16,32,256]{3,2,1,0:T(8,128)S(1)}, f32[2,16,32,256]{3,2,1,0:T(8,128)S(1)}, u32[]{:S(2)}, u32[]{:S(2)}) collective-permute-start(f32[2,16,32,256]{3,2,1,0:T(8,128)S(1)} %bitcast.22), channel_id=1, source_target_pairs={{2,0},{9,1},{6,2},{19,3},{0,4},{21,5},{4,6},{15,7},{12,8},{25,9},{... | collective-permute-start | bytes 3145736 | tf_op jit(solution)/shard_map/ppermute | solution.py:196
  35.3 0.9 collective-permute-done.8
  36.2 2.6 %collective-permute-start.9 = (f32[2,16,256]{2,1,0:T(8,128)S(1)}, f32[2,16,256]{2,1,0:T(8,128)S(1)}, u32[]{:S(2)}, u32[]{:S(2)}) collective-permute-start(f32[2,16,256]{2,1,0:T(8,128)S(1)} %broadcast_multiply_fusion.mean0), channel_id=1, source_target_pairs={{0,1},{1,0},{2,3},{3,2},{4,5},{5,4},{6,7},{7,6},{8,9},{9,8},{10,11... | collective-permute-start | bytes 98312 | tf_op jit(solution)/shard_map/ppermute | solution.py:45
  38.8 1.9 %fusion.10 = (f32[256,128]{1,0:T(8,128)S(1)}, f32[256,128]{1,0:T(8,128)S(1)}, f32[256,128]{1,0:T(8,128)}, f32[256,128]{1,0:T(8,128)}) fusion(s32[128]{0:T(128)S(1)} %iota_add_fusion.2, s32[256]{0:T(256)S(1)} %iota_add_fusion.1, s32[256]{0:T(256)S(1)} %iota_add_fusion), kind=kLoop, calls=%fused_computation.37 | loop fusion | flops 917504 | bytes 526848 | tf_op jit(solution)/shard_map/sin | solution.py:53
  40.7 0.9 collective-permute-start.11
  41.6 1.7 %collective-permute-done.6.own1_im = f32[16,32,256]{2,1,0:T(8,128)S(1)} collective-permute-done((f32[16,32,256]{2,1,0:T(8,128)}, f32[16,32,256]{2,1,0:T(8,128)S(1)}, u32[]{:S(2)}, u32[]{:S(2)}) %collective-permute-start.6) | collective-permute-done | bytes 524320 | tf_op jit(solution)/shard_map/ppermute | solution.py:45
  43.2 0.4 collective-permute-done.9.mean1
  43.6 2.0 %collective-permute-start.12 = (f32[16,32,256]{2,1,0:T(8,128)S(1)}, f32[16,32,256]{2,1,0:T(8,128)}, u32[]{:S(2)}, u32[]{:S(2)}) collective-permute-start(f32[16,32,256]{2,1,0:T(8,128)S(1)} %collective-permute-done.6.own1_im), channel_id=1, source_target_pairs={{2,0},{9,1},{6,2},{19,3},{0,4},{21,5},{4,6},{15,7},{12,8},{25,9},{... | collective-permute-start | bytes 1572872 | tf_op jit(solution)/shard_map/ppermute | solution.py:196
  45.5 0.1 pad_add_fusion
  45.6 0.8 dynamic-slice_convert_fusion
  46.5 1.1 %reduce-precision_convert_fusion = (bf16[512,128]{1,0:T(8,128)(2,1)S(1)}, bf16[512,128]{1,0:T(8,128)(2,1)S(1)}, bf16[512,128]{1,0:T(8,128)(2,1)S(1)}, bf16[512,128]{1,0:T(8,128)(2,1)S(1)}) fusion(f32[256,128]{1,0:T(8,128)} %get-tuple-element.42, f32[256,128]{1,0:T(8,128)S(1)} %get-tuple-element.37, f32[256,128]{1,0:T(8,128)} %get-tuple-element.41, ...), kind=kLoop, calls=%fused_computation.4 | loop fusion | flops 655360 | bytes 1048576 | tf_op jit(solution)/shard_map/convert_element_type | solution.py:58
  47.6 8.3 %collective-permute-done.11.far1_re = f32[16,32,256]{2,1,0:T(8,128)} collective-permute-done((f32[16,32,256]{2,1,0:T(8,128)S(1)}, f32[16,32,256]{2,1,0:T(8,128)}, u32[]{:S(2)}, u32[]{:S(2)}) %collective-permute-start.11) | collective-permute-done | bytes 524320 | tf_op jit(solution)/shard_map/ppermute | solution.py:196
  55.9 0.0 collective-permute-done.10.far0
  55.9 5.6 %collective-permute-done.12.far1_im = f32[16,32,256]{2,1,0:T(8,128)} collective-permute-done((f32[16,32,256]{2,1,0:T(8,128)S(1)}, f32[16,32,256]{2,1,0:T(8,128)}, u32[]{:S(2)}, u32[]{:S(2)}) %collective-permute-start.12) | collective-permute-done | bytes 524320 | tf_op jit(solution)/shard_map/ppermute | solution.py:196
  61.5 0.1 broadcast_in_dim.19.own_n
  61.6 0.1 broadcast_in_dim.20.far_n
  61.6 8.5 %edge.2 = (f32[16,16,128]{2,1,0:T(8,128)S(1)}, f32[16,16,128]{2,1,0:T(8,128)S(1)}, f32[16,32,128]{2,1,0:T(8,128)S(1)}) custom-call(s32[2]{0:T(128)S(1)} %get-tuple-element.43.place, f32[2,16,32,256]{3,2,1,0:T(8,128)S(1)} %bitcast.23, f32[16,32,256]{2,1,0:T(8,128)S(1)} %collective-permute-done.1.own1_re, f32[16,32,256]{2,1,0:T(8,128)S(1)} %collective-permute-done.6.own1_im, ...), custom_call_target="tpu_custom_call" | custom-call | flops 800000000 | bytes 5000000 | tf_op jit(solution)/shard_map/edge/pallas_call | solution.py:162
  70.2 3.0 %collective-permute-start.13 = (f32[16,32,128]{2,1,0:T(8,128)S(1)}, f32[16,32,128]{2,1,0:T(8,128)S(1)}, u32[]{:S(2)}, u32[]{:S(2)}) collective-permute-start(f32[16,32,128]{2,1,0:T(8,128)S(1)} %get-tuple-element.25), channel_id=1, source_target_pairs={{0,3},{1,8},{2,7},{3,18},{4,1},{5,20},{6,5},{7,14},{8,13},{9,24},{... | collective-permute-start | bytes 786440 | tf_op jit(solution)/shard_map/ppermute | solution.py:192
  73.2 0.0 collective-permute-start.14
  73.2 8.5 %edge.3 = (f32[16,16,128]{2,1,0:T(8,128)S(1)}, f32[16,16,128]{2,1,0:T(8,128)S(1)}, f32[16,32,128]{2,1,0:T(8,128)S(1)}) custom-call(s32[2]{0:T(128)S(1)} %get-tuple-element.44.place, f32[2,16,32,256]{3,2,1,0:T(8,128)S(1)} %bitcast.24, f32[16,32,256]{2,1,0:T(8,128)S(1)} %collective-permute-done.1.own1_re, f32[16,32,256]{2,1,0:T(8,128)S(1)} %collective-permute-done.6.own1_im, ...), custom_call_target="tpu_custom_call" | custom-call | flops 800000000 | bytes 5000000 | tf_op jit(solution)/shard_map/edge/pallas_call | solution.py:162
  81.7 3.6 %collective-permute-start.15 = (f32[16,16,128]{2,1,0:T(8,128)S(1)}, f32[16,16,128]{2,1,0:T(8,128)S(1)}, u32[]{:S(2)}, u32[]{:S(2)}) collective-permute-start(f32[16,16,128]{2,1,0:T(8,128)S(1)} %get-tuple-element.27), channel_id=1, source_target_pairs={{0,1},{1,0},{2,3},{3,2},{4,5},{5,4},{6,7},{7,6},{8,9},{9,8},{10,11... | collective-permute-start | bytes 393224 | tf_op jit(solution)/shard_map/ppermute | solution.py:45
  85.4 0.2 collective-permute-start.16
  85.6 0.1 broadcast_in_dim.18
  85.7 0.0 collective-permute-done.13
  85.8 0.0 collective-permute-done.14
  85.8 2.5 %collective-permute-done.15 = f32[16,16,128]{2,1,0:T(8,128)S(1)} collective-permute-done((f32[16,16,128]{2,1,0:T(8,128)S(1)}, f32[16,16,128]{2,1,0:T(8,128)S(1)}, u32[]{:S(2)}, u32[]{:S(2)}) %collective-permute-start.15) | collective-permute-done | bytes 131104 | tf_op jit(solution)/shard_map/ppermute | solution.py:45
  88.3 0.0 copy-start.1
  88.3 3.4 %collective-permute-done.16 = f32[16,32,128]{2,1,0:T(8,128)S(1)} collective-permute-done((f32[16,32,128]{2,1,0:T(8,128)S(1)}, f32[16,32,128]{2,1,0:T(8,128)S(1)}, u32[]{:S(2)}, u32[]{:S(2)}) %collective-permute-start.16) | collective-permute-done | bytes 262176 | tf_op jit(solution)/shard_map/ppermute | solution.py:192
  91.7 0.0 copy-done.1
  91.7 0.7 bitcast_dynamic-update-slice_fusion
  (18 shorter events, 0.2 us)
Async XLA Ops:
  0.0 2.3 %copy-start = (f32[32,2,16,256]{3,2,1,0:T(8,128)S(1)}, f32[32,2,16,256]{3,2,1,0:T(8,128)}, u32[]{:S(2)}) copy-start(f32[32,2,16,256]{3,2,1,0:T(8,128)} %param.2) | copy-start | bytes 3145732
  1.4 4.0 %collective-permute-start = (f32[2,16,256]{2,1,0:T(8,128)S(1)}, f32[2,16,256]{2,1,0:T(8,128)S(1)}, u32[]{:S(2)}, u32[]{:S(2)}) collective-permute-start(f32[2,16,256]{2,1,0:T(8,128)S(1)} %reduce_sum.9), channel_id=1, source_target_pairs={{0,128},{2,130},{4,132},{6,134},{8,136},{10,138},{12,140},{14,142}... | collective-permute-start | bytes 98312 | tf_op jit(solution)/shard_map/ppermute | solution.py:41
  6.3 20.5 %collective-permute-start.1 = (f32[16,32,256]{2,1,0:T(8,128)S(1)}, f32[16,32,256]{2,1,0:T(8,128)S(1)}, u32[]{:S(2)}, u32[]{:S(2)}) collective-permute-start(f32[16,32,256]{2,1,0:T(8,128)S(1)} %get-tuple-element.30), channel_id=1, source_target_pairs={{0,1},{1,0},{2,3},{3,2},{4,5},{5,4},{6,7},{7,6},{8,9},{9,8},{10,11... | collective-permute-start | bytes 1572872 | tf_op jit(solution)/shard_map/ppermute | solution.py:45
  8.0 1.2 %collective-permute-start.2 = (f32[2,16,256]{2,1,0:T(8,128)S(1)}, f32[2,16,256]{2,1,0:T(8,128)S(1)}, u32[]{:S(2)}, u32[]{:S(2)}) collective-permute-start(f32[2,16,256]{2,1,0:T(8,128)S(1)} %add.104), channel_id=1, source_target_pairs={{0,2},{2,0},{4,6},{6,4},{8,10},{10,8},{12,14},{14,12},{16,18},{18,... | collective-permute-start | bytes 98312 | tf_op jit(solution)/shard_map/ppermute | solution.py:41
  9.2 3.9 %collective-permute-start.3 = (f32[2,16,256]{2,1,0:T(8,128)S(1)}, f32[2,16,256]{2,1,0:T(8,128)S(1)}, u32[]{:S(2)}, u32[]{:S(2)}) collective-permute-start(f32[2,16,256]{2,1,0:T(8,128)S(1)} %add.105), channel_id=1, source_target_pairs={{0,16},{2,18},{4,20},{6,22},{8,24},{10,26},{12,28},{14,30},{16,0},... | collective-permute-start | bytes 98312 | tf_op jit(solution)/shard_map/ppermute | solution.py:41
  13.1 5.2 %collective-permute-start.4 = (f32[2,16,256]{2,1,0:T(8,128)S(1)}, f32[2,16,256]{2,1,0:T(8,128)S(1)}, u32[]{:S(2)}, u32[]{:S(2)}) collective-permute-start(f32[2,16,256]{2,1,0:T(8,128)S(1)} %add.106), channel_id=1, source_target_pairs={{0,32},{2,34},{4,36},{6,38},{8,40},{10,42},{12,44},{14,46},{16,48}... | collective-permute-start | bytes 98312 | tf_op jit(solution)/shard_map/ppermute | solution.py:41
  18.3 8.4 %collective-permute-start.5 = (f32[2,16,256]{2,1,0:T(8,128)S(1)}, f32[2,16,256]{2,1,0:T(8,128)S(1)}, u32[]{:S(2)}, u32[]{:S(2)}) collective-permute-start(f32[2,16,256]{2,1,0:T(8,128)S(1)} %add.107), channel_id=1, source_target_pairs={{0,64},{2,66},{4,68},{6,70},{8,72},{10,74},{12,76},{14,78},{16,80}... | collective-permute-start | bytes 98312 | tf_op jit(solution)/shard_map/ppermute | solution.py:41
  26.8 5.5 %collective-permute-start.7 = (f32[2,16,256]{2,1,0:T(8,128)S(1)}, f32[2,16,256]{2,1,0:T(8,128)S(1)}, u32[]{:S(2)}, u32[]{:S(2)}) collective-permute-start(f32[2,16,256]{2,1,0:T(8,128)S(1)} %add.108), channel_id=1, source_target_pairs={{0,8},{2,10},{4,12},{6,14},{8,0},{10,2},{12,4},{14,6},{16,24},{18,... | collective-permute-start | bytes 98312 | tf_op jit(solution)/shard_map/ppermute | solution.py:41
  30.0 13.2 %collective-permute-start.6 = (f32[16,32,256]{2,1,0:T(8,128)}, f32[16,32,256]{2,1,0:T(8,128)S(1)}, u32[]{:S(2)}, u32[]{:S(2)}) collective-permute-start(f32[16,32,256]{2,1,0:T(8,128)} %get-tuple-element.29), channel_id=1, source_target_pairs={{0,1},{1,0},{2,3},{3,2},{4,5},{5,4},{6,7},{7,6},{8,9},{9,8},{10,11... | collective-permute-start | bytes 1572872 | tf_op jit(solution)/shard_map/ppermute | solution.py:45
  32.3 4.0 %collective-permute-start.8 = (f32[2,16,256]{2,1,0:T(8,128)S(1)}, f32[2,16,256]{2,1,0:T(8,128)S(1)}, u32[]{:S(2)}, u32[]{:S(2)}) collective-permute-start(f32[2,16,256]{2,1,0:T(8,128)S(1)} %add.109), channel_id=1, source_target_pairs={{0,4},{2,6},{4,0},{6,2},{8,12},{10,14},{12,8},{14,10},{16,20},{18,... | collective-permute-start | bytes 98312 | tf_op jit(solution)/shard_map/ppermute | solution.py:41
  33.9 22.0 %collective-permute-start.10 = (f32[2,16,32,256]{3,2,1,0:T(8,128)S(1)}, f32[2,16,32,256]{3,2,1,0:T(8,128)S(1)}, u32[]{:S(2)}, u32[]{:S(2)}) collective-permute-start(f32[2,16,32,256]{3,2,1,0:T(8,128)S(1)} %bitcast.22), channel_id=1, source_target_pairs={{2,0},{9,1},{6,2},{19,3},{0,4},{21,5},{4,6},{15,7},{12,8},{25,9},{... | collective-permute-start | bytes 3145736 | tf_op jit(solution)/shard_map/ppermute | solution.py:196
  36.2 7.4 %collective-permute-start.9 = (f32[2,16,256]{2,1,0:T(8,128)S(1)}, f32[2,16,256]{2,1,0:T(8,128)S(1)}, u32[]{:S(2)}, u32[]{:S(2)}) collective-permute-start(f32[2,16,256]{2,1,0:T(8,128)S(1)} %broadcast_multiply_fusion.mean0), channel_id=1, source_target_pairs={{0,1},{1,0},{2,3},{3,2},{4,5},{5,4},{6,7},{7,6},{8,9},{9,8},{10,11... | collective-permute-start | bytes 98312 | tf_op jit(solution)/shard_map/ppermute | solution.py:45
  40.7 15.1 %collective-permute-start.11 = (f32[16,32,256]{2,1,0:T(8,128)S(1)}, f32[16,32,256]{2,1,0:T(8,128)}, u32[]{:S(2)}, u32[]{:S(2)}) collective-permute-start(f32[16,32,256]{2,1,0:T(8,128)S(1)} %collective-permute-done.1.own1_re), channel_id=1, source_target_pairs={{2,0},{9,1},{6,2},{19,3},{0,4},{21,5},{4,6},{15,7},{12,8},{25,9},{... | collective-permute-start | bytes 1572872 | tf_op jit(solution)/shard_map/ppermute | solution.py:196
  43.6 17.9 %collective-permute-start.12 = (f32[16,32,256]{2,1,0:T(8,128)S(1)}, f32[16,32,256]{2,1,0:T(8,128)}, u32[]{:S(2)}, u32[]{:S(2)}) collective-permute-start(f32[16,32,256]{2,1,0:T(8,128)S(1)} %collective-permute-done.6.own1_im), channel_id=1, source_target_pairs={{2,0},{9,1},{6,2},{19,3},{0,4},{21,5},{4,6},{15,7},{12,8},{25,9},{... | collective-permute-start | bytes 1572872 | tf_op jit(solution)/shard_map/ppermute | solution.py:196
  70.2 15.6 %collective-permute-start.13 = (f32[16,32,128]{2,1,0:T(8,128)S(1)}, f32[16,32,128]{2,1,0:T(8,128)S(1)}, u32[]{:S(2)}, u32[]{:S(2)}) collective-permute-start(f32[16,32,128]{2,1,0:T(8,128)S(1)} %get-tuple-element.25), channel_id=1, source_target_pairs={{0,3},{1,8},{2,7},{3,18},{4,1},{5,20},{6,5},{7,14},{8,13},{9,24},{... | collective-permute-start | bytes 786440 | tf_op jit(solution)/shard_map/ppermute | solution.py:192
  73.2 12.6 %collective-permute-start.14 = (f32[16,16,128]{2,1,0:T(8,128)S(1)}, f32[16,16,128]{2,1,0:T(8,128)S(1)}, u32[]{:S(2)}, u32[]{:S(2)}) collective-permute-start(f32[16,16,128]{2,1,0:T(8,128)S(1)} %get-tuple-element.26), channel_id=1, source_target_pairs={{0,1},{1,0},{2,3},{3,2},{4,5},{5,4},{6,7},{7,6},{8,9},{9,8},{10,11... | collective-permute-start | bytes 393224 | tf_op jit(solution)/shard_map/ppermute | solution.py:45
  81.7 6.6 %collective-permute-start.15 = (f32[16,16,128]{2,1,0:T(8,128)S(1)}, f32[16,16,128]{2,1,0:T(8,128)S(1)}, u32[]{:S(2)}, u32[]{:S(2)}) collective-permute-start(f32[16,16,128]{2,1,0:T(8,128)S(1)} %get-tuple-element.27), channel_id=1, source_target_pairs={{0,1},{1,0},{2,3},{3,2},{4,5},{5,4},{6,7},{7,6},{8,9},{9,8},{10,11... | collective-permute-start | bytes 393224 | tf_op jit(solution)/shard_map/ppermute | solution.py:45
  85.4 6.4 %collective-permute-start.16 = (f32[16,32,128]{2,1,0:T(8,128)S(1)}, f32[16,32,128]{2,1,0:T(8,128)S(1)}, u32[]{:S(2)}, u32[]{:S(2)}) collective-permute-start(f32[16,32,128]{2,1,0:T(8,128)S(1)} %get-tuple-element.28), channel_id=1, source_target_pairs={{0,2},{1,9},{2,6},{3,19},{4,0},{5,21},{6,4},{7,15},{8,12},{9,25},{... | collective-permute-start | bytes 786440 | tf_op jit(solution)/shard_map/ppermute | solution.py:192
  88.3 3.4 %copy-start.1 = (f32[4,16,32,128]{3,2,1,0:T(8,128)}, f32[4,16,32,128]{3,2,1,0:T(8,128)S(1)}, u32[]{:S(2)}) copy-start(f32[4,16,32,128]{3,2,1,0:T(8,128)S(1)} %bitcast_dynamic-update-slice_fusion.2) | copy-start | bytes 3145732

commit v2 on v1

v2 whole, which is shorter than its diff:
```python
import functools
import math

import jax
import jax.numpy as jnp
import ml_dtypes
import numpy as np
from jax import lax
from jax.experimental import pallas as pl
from jax.experimental.pallas import tpu as pltpu
from jax.sharding import PartitionSpec as P

F32 = jnp.float32
BF16 = jnp.bfloat16
FBAND = 512
NFFT = 8192
K0 = 164
LAGS = 128
ROUNDS = 4
WINDOWS = 16
CHANNELS = 4096
A_TILE = 4
LANE = 128


def parity_of(index):
    return (index ^ (index >> 1) ^ (index >> 2) ^ (index >> 3)) & 1


def owner_round(parity, freq):
    return 2 * parity + freq


def edge_route(chan_count, flip):
    route = []
    for chan in range(chan_count):
        for freq in range(2):
            far = chan ^ (1 << owner_round(parity_of(chan), freq))
            route.append((chan * 2 + freq, far * 2 + (freq ^ flip)))
    return route


def from_chan(block, source, chan_count):
    return lax.ppermute(block, "chan", [(source(i), i) for i in range(chan_count)])


def step_y(chan, by):
    return (chan & ~6) | (((chan >> 1) + by) % 4 << 1)


def step_z(chan, by):
    return (chan & ~56) | (((chan >> 3) + by) % 8 << 3)


def sum_over_chan(sums, size, order, hooks):
    top = size // 2
    steps = {
        "core": [lambda i: i ^ 1],
        "z1": [lambda i: i ^ 8],
        "z": [lambda i: step_z(i, 4), lambda i: step_z(i, 2), lambda i: step_z(i, -2)],
        "y": [lambda i: step_y(i, 2), lambda i: step_y(i, 1), lambda i: step_y(i, -1)],
        "y2": [lambda i: i ^ 4],
        "y1": [lambda i: i ^ 2],
    }
    for name in order:
        sums = sum((from_chan(sums, source, size) for source in steps[name]), sums)
        sums = lax.optimization_barrier(sums)
        if name in hooks:
            sums = hooks[name](sums)
    far = swap_freq(sums)
    near = from_chan(sums, lambda i: i ^ top, size)
    diagonal = lax.ppermute(
        sums, ("chan", "freq"), [(d, d ^ (2 * top) ^ 1) for d in range(2 * size)]
    )
    return sums, near, far, diagonal


def swap_freq(block):
    return lax.ppermute(block, "freq", [(0, 1), (1, 0)])


def lag_tables():
    bins = K0 + np.arange(FBAND)
    lags = np.arange(LAGS) - LAGS // 2
    angles = (bins[:, None] * lags[None, :] % NFFT) * (2.0 * math.pi / NFFT)
    tables = []
    for table in (np.cos(angles), np.sin(angles)):
        high = table.astype(ml_dtypes.bfloat16)
        low = (table - high.astype(np.float64)).astype(ml_dtypes.bfloat16)
        tables.append(np.concatenate([high, low], axis=1))
    return tables


def channel_counts(windows, chan, chans):
    per_row = LANE // chans
    row = windows[pl.ds(chan // per_row, 1), :]
    lanes = lax.broadcasted_iota(jnp.int32, (chans, LANE), 1)
    first = lax.broadcasted_iota(jnp.int32, (chans, LANE), 0) + chan % per_row * chans
    picked = jnp.where(lanes == first, row, 0).astype(F32)
    return jnp.sum(picked, axis=1, keepdims=True)


def means(sums):
    sum0, near0, sum1, near1 = sums
    return [
        (total[part] + near[part]) * (1.0 / CHANNELS)
        for total, near in ((sum0, near0), (sum1, near1))
        for part in range(2)
    ]


def whiten(low, high, mean, count):
    re0, im0 = low[0] - mean[0], low[1] - mean[1]
    re1, im1 = high[0] - mean[2], high[1] - mean[3]
    energy = jnp.sum(re0 * re0 + im0 * im0 + re1 * re1 + im1 * im1, axis=1, keepdims=True)
    scale = lax.rsqrt(energy * (1.0 / FBAND) + 1e-06)
    window = lax.broadcasted_iota(jnp.int32, (WINDOWS, LANE), 0).astype(F32)
    scale = jnp.where(window < count, scale, 0.0)
    re, im = [], []
    for real, imag in ((re0, im0), (re1, im1)):
        for lane in range(0, real.shape[1], LANE):
            re.append(real[:, lane : lane + LANE] * scale)
            im.append(imag[:, lane : lane + LANE] * scale)
    return re, im


def own_body(
    place, raw, other, sum0, near0, sum1, near1, windows, all_tables,
    a_rows, table, own_n, far_n, buf, sem, table_sem,
):
    chans, _, _, half = raw.shape
    step = 8
    fetches = []
    for c in range(chans // step):
        at = pl.ds(c * step, step)
        for k, source in enumerate((raw, other)):
            fetches.append(pltpu.make_async_copy(source.at[at], buf.at[k, at], sem.at[k, c]))
    for fetch in fetches:
        fetch.start()
    first_bin = pl.multiple_of(place[1] * (half // (chans // 2)), half)
    table_fetch = pltpu.make_async_copy(
        all_tables.at[:, pl.ds(first_bin, 2 * half), :], table, table_sem
    )
    table_fetch.start()
    own_n[...] = jnp.broadcast_to(channel_counts(windows, place[2], chans), (chans, LANE))
    far_n[...] = jnp.broadcast_to(channel_counts(windows, place[3], chans), (chans, LANE))
    mean = means((sum0, near0, sum1, near1))
    for c in range(chans // step):
        fetches[2 * c].wait()
        fetches[2 * c + 1].wait()

        def channel(k, carry):
            a = c * step + k
            re, im = whiten(buf[0, a], buf[1, a], mean, own_n[pl.ds(a, 1), :])
            for lane, (v, u) in enumerate(zip(re, im)):
                for plane, value in enumerate((v, u, v + u)):
                    first = pl.multiple_of(a * (3 * WINDOWS) + plane * WINDOWS, WINDOWS)
                    a_rows[lane, pl.ds(first, WINDOWS), :] = value
            return carry

        lax.fori_loop(0, step, channel, 0, unroll=True)
    table_fetch.wait()


def whiten_own(place, raw, other, sums, windows, all_tables):
    chans, _, _, half = raw.shape
    vmem = pl.BlockSpec(memory_space=pltpu.VMEM)
    anywhere = pl.BlockSpec(memory_space=pl.ANY)
    counts = jax.ShapeDtypeStruct((chans, LANE), F32)
    return pl.pallas_call(
        own_body,
        out_shape=(
            jax.ShapeDtypeStruct((2 * half // LANE, chans * 3 * WINDOWS, LANE), F32),
            jax.ShapeDtypeStruct((2, 2 * half, 2 * LAGS), BF16),
            counts,
            counts,
        ),
        in_specs=[pl.BlockSpec(memory_space=pltpu.SMEM)] + [anywhere] * 2 + [vmem] * 5 + [anywhere],
        out_specs=(vmem, vmem, vmem, vmem),
        scratch_shapes=[
            pltpu.VMEM((2, *raw.shape), F32),
            pltpu.SemaphoreType.DMA((2, chans // 8)),
            pltpu.SemaphoreType.DMA,
        ],
        compiler_params=pltpu.CompilerParams(vmem_limit_bytes=12 * 1024 * 1024),
        name="own",
    )(place, raw, other, *sums, windows, all_tables)


def edge_body(first, place, a_rows, far0, far1, table, sum0, near0, sum1, near1, own_n, far_n, *refs):
    if first:
        keep_ref, other_ref, far_ref, b_rows, g_high, g_low, far_buf, sem = refs
    else:
        keep1, other1, keep_ref, other_ref, far_ref, b_rows, g_high, g_low, far_buf, sem = refs
    chans, _, _, half = far0.shape
    hrows = chans // 2
    b0 = pl.multiple_of(place[0], hrows)
    a_keep = place[1]
    b_rows_at = pl.ds(b0, hrows)
    fetches = [
        pltpu.make_async_copy(source.at[b_rows_at], far_buf.at[k], sem.at[k])
        for k, source in enumerate((far0, far1))
    ]
    for fetch in fetches:
        fetch.start()
    mean = means((sum0, near0, sum1, near1))
    for fetch in fetches:
        fetch.wait()

    def channel(b, carry):
        re, im = whiten(far_buf[0, b], far_buf[1, b], mean, far_n[pl.ds(b0 + b, 1), :])
        for lane, (v, u) in enumerate(zip(re, im)):
            for plane, value in enumerate((v + u, u - v, v)):
                at = pl.ds(plane * WINDOWS * hrows + b, WINDOWS, stride=hrows)
                b_rows[lane, at, :] = value
        return carry

    lax.fori_loop(0, hrows, channel, 0, unroll=True)

    def products(t, carry):
        a0 = t * A_TILE
        for c in range(2 * half // LANE):
            sums = [[None] * 3 for _ in range(A_TILE)]
            for w in range(WINDOWS):
                far = [
                    b_rows[c, pl.ds((k * WINDOWS + w) * hrows, hrows), :] for k in range(3)
                ]
                for j in range(A_TILE):
                    for k in range(3):
                        own = a_rows[c, pl.ds((a0 + j) * (3 * WINDOWS) + k * WINDOWS + w, 1), :]
                        term = own * far[k]
                        sums[j][k] = term if w == 0 else sums[j][k] + term
            for j in range(A_TILE):
                s_im, s_re, s_both = sums[j]
                rows = pl.ds(pl.multiple_of((a0 + j) * hrows, hrows), hrows)
                for part, value in enumerate((s_both + s_re, s_both - s_im)):
                    high = value.astype(BF16)
                    at = slice(part * 2 * half + c * LANE, part * 2 * half + (c + 1) * LANE)
                    g_high[rows, at] = high
                    g_low[rows, at] = (value - high.astype(F32)).astype(BF16)
        return carry

    lax.fori_loop(0, chans // A_TILE, products, 0)
    far_counts = far_n[pl.ds(b0, hrows), :]
    group = 8

    def lagged(t, carry):
        size = group * hrows
        rows = pl.ds(pl.multiple_of(t * size, size), size)

        def project(part):
            at = slice(2 * part * half, 2 * (part + 1) * half)
            both = jnp.dot(g_high[rows, at], table[part], preferred_element_type=F32)
            low = jnp.dot(g_low[rows, at], table[part, :, :LAGS], preferred_element_type=F32)
            return both[:, :LAGS] + both[:, LAGS:] + low

        real = project(0)
        imag = project(1)
        forward = real - imag
        backward = real + imag
        for j in range(group):
            a = t * group + j
            shared = jnp.minimum(far_counts, own_n[pl.ds(a, 1), :])
            scale = (1.0 / math.sqrt(FBAND)) / shared
            at = slice(j * hrows, (j + 1) * hrows)
            far_ref[:, a, :] = backward[at] * scale
            value = forward[at] * scale
            mine = (a >= a_keep) & (a < a_keep + hrows)

            spot = slice(None) if first else b_rows_at

            @pl.when(mine)
            def _():
                keep_ref[a - a_keep, spot, :] = value

            @pl.when(jnp.logical_not(mine))
            def _():
                other_ref[a - (hrows - a_keep), spot, :] = value

        return carry

    lax.fori_loop(0, chans // group, lagged, 0)
    if not first:
        before = pl.ds(pl.multiple_of(hrows - b0, hrows), hrows)
        keep_ref[:, before, :] = keep1[...]
        other_ref[:, before, :] = other1[...]


def edge(place, a_rows, far, table, sums, counts, before=()):
    chans, _, _, half = far[0].shape
    band = 2 * half
    hrows = chans // 2
    vmem = pl.BlockSpec(memory_space=pltpu.VMEM)
    anywhere = pl.BlockSpec(memory_space=pl.ANY)
    mine = jax.ShapeDtypeStruct((hrows, chans if before else hrows, LAGS), F32)
    return pl.pallas_call(
        functools.partial(edge_body, not before),
        out_shape=(mine, mine, jax.ShapeDtypeStruct((hrows, chans, LAGS), F32)),
        in_specs=[pl.BlockSpec(memory_space=pltpu.SMEM), vmem]
        + [anywhere] * 2 + [vmem] * (7 + len(before)),
        out_specs=(vmem, vmem, vmem),
        scratch_shapes=[
            pltpu.VMEM((band // LANE, 3 * WINDOWS * hrows, LANE), F32),
            pltpu.VMEM((chans * hrows, 2 * band), BF16),
            pltpu.VMEM((chans * hrows, 2 * band), BF16),
            pltpu.VMEM((2, hrows, 2, WINDOWS, half), F32),
            pltpu.SemaphoreType.DMA((2,)),
        ],
        compiler_params=pltpu.CompilerParams(vmem_limit_bytes=20 * 1024 * 1024),
        cost_estimate=pl.CostEstimate(flops=1_000_000, bytes_accessed=10_000, transcendentals=0),
        name="edge",
    )(place, a_rows, *far, table, *sums, *counts, *before)


def on_device(raw_spectra, valid_windows):
    chans, _, _, half = raw_spectra.shape
    hrows = chans // 2
    size = lax.axis_size("chan")
    chan_index = lax.axis_index("chan")
    freq_index = lax.axis_index("freq")
    barrier = lax.optimization_barrier

    def to_partner(block, flip):
        return lax.ppermute(block, ("chan", "freq"), edge_route(size, flip))

    def from_partner(block):
        route = [(high, low) for low, high in edge_route(size, 0)]
        return lax.ppermute(block, ("chan", "freq"), route)

    parity = parity_of(chan_index)
    my_round = owner_round(parity, freq_index)
    partner = chan_index ^ (1 << my_round)

    sums = jnp.sum(raw_spectra, axis=0)
    other = swap_freq(raw_spectra)
    far = {}

    def after_z1(sums):
        held, sums = barrier((raw_spectra, sums))
        far["mine"] = from_partner(held)
        return sums

    def after_core(sums):
        far["own"], far["mine"], sums = barrier((other, far["mine"], sums))
        far["other"] = from_partner(far["own"])
        return sums

    sums = sum_over_chan(
        sums, size, ("z1", "z", "y", "core"), {"z1": after_z1, "core": after_core}
    )
    windows = valid_windows.reshape(-1, LANE)

    def at(b0):
        return jnp.stack([b0, freq_index * hrows, chan_index, partner]).astype(jnp.int32)

    all_tables = np.stack(lag_tables())
    all_tables = jnp.asarray(np.concatenate([all_tables, all_tables[:, :half]], axis=1))
    a_rows, table, *counts = whiten_own(at(0), raw_spectra, far["own"], sums, windows, all_tables)

    def work(b0, before=()):
        return edge(at(b0), a_rows, (far["mine"], far["other"]), table, sums, counts, before)

    keep, other, far1 = work((1 - freq_index) * hrows)
    far1 = to_partner(far1, 1)
    keep, other, far2 = work(freq_index * hrows, (keep, other))
    other = swap_freq(other)
    far1, far2 = barrier((far1, far2))
    far2 = to_partner(far2, 0)

    index = lax.broadcasted_iota(jnp.int32, (ROUNDS, 1, 1, 1), 0)
    own_pair = index // 2 == parity
    same_freq = index % 2 == freq_index
    return jnp.where(
        own_pair, jnp.where(same_freq, keep, other), jnp.where(same_freq, far2, far1)
    )


def solution(mesh):
    return jax.shard_map(
        on_device,
        mesh=mesh,
        in_specs=(P("chan", None, None, "freq"), P()),
        out_specs=P(None, ("chan", "freq"), None, None),
        check_vma=False,
    )
```

time: 92.7 us -> 84 us (0.906)
  the two profiles are of different devices: /device:TPU:6 before, /device:TPU:1 now
where the time goes in v2:
time: 84 us; the launch traced here: 83.7 us
  starting transfers between devices  42.9 us (51%)
  waiting for transfers between devices  18.5 us (22%)
  Pallas kernels  16.5 us (20%)
  local copies, waits for them, and re-layouts  3.08 us (4%)
  other arithmetic  2.7 us (3%)
    ppermute x9, starting transfers between devices, from_chan(): lax.ppermute(block, 'chan', [(source(i), i) for i in range(chan_count)])  21.7 us
    pallas_call x2, Pallas kernels, edge(): pl.pallas_call(functools.partial(edge_body, not before), out_shape=(mine,...  15 us
    ppermute x3, waiting for transfers between devices, swap_freq(): return lax.ppermute(block, 'freq', [(0, 1), (1, 0)])  11.3 us
    ppermute x1, starting transfers between devices, sum_over_chan(): lax.ppermute(sums, ('chan', 'freq'), [(d, d ^ 2 * top ^ 1) for d in range...  7.96 us
    ppermute x2, starting transfers between devices, to_partner(): return lax.ppermute(block, ('chan', 'freq'), edge_route(size, flip))  7.62 us
    ppermute x9, waiting for transfers between devices, from_chan(): lax.ppermute(block, 'chan', [(source(i), i) for i in range(chan_count)])  6.65 us
    ppermute x3, starting transfers between devices, swap_freq(): return lax.ppermute(block, 'freq', [(0, 1), (1, 0)])  3.2 us
    unnamed x6, local copies, waits for them, and re-layouts  3.08 us
  transfers between devices with their start and end apart: 17, of which 7 were waited for; matrix products, arithmetic and copies ran while one was open for 0% of the time, Pallas kernels for 11%

profile of v2, /device:TPU:1, one launch (start us, length us, event | category | flops | bytes accessed | tf_op | source)
XLA Modules:
  0.0 83.7 jit_solution(1606557124057046725)
XLA Ops:
  0.0 1.3 %reduce_sum.9 = f32[2,16,256]{2,1,0:T(8,128)S(1)} reduce(f32[32,2,16,256]{3,2,1,0:T(8,128)} %raw.1, f32[]{:T(128)} %constant.47.clone.1), dimensions={0}, to_apply=%region_0.0 | reduce | flops 253952 | bytes 1081348 | tf_op jit(solution)/shard_map/reduce_sum | solution.py:334
  1.3 2.6 %collective-permute-start.1 = (f32[2,16,256]{2,1,0:T(8,128)S(1)}, f32[2,16,256]{2,1,0:T(8,128)S(1)}, u32[]{:S(2)}, u32[]{:S(2)}) collective-permute-start(f32[2,16,256]{2,1,0:T(8,128)S(1)} %reduce_sum.9), channel_id=1, source_target_pairs={{16,0},{18,2},{20,4},{22,6},{24,8},{26,10},{28,12},{30,14},{0,16},... | collective-permute-start | bytes 98312 | tf_op jit(solution)/shard_map/ppermute | solution.py:44
  3.9 2.7 %collective-permute-start = (f32[32,2,16,256]{3,2,1,0:T(8,128)}, f32[32,2,16,256]{3,2,1,0:T(8,128)S(1)}, u32[]{:S(2)}, u32[]{:S(2)}) collective-permute-start(f32[32,2,16,256]{3,2,1,0:T(8,128)} %raw.1), channel_id=1, source_target_pairs={{0,1},{1,0},{2,3},{3,2},{4,5},{5,4},{6,7},{7,6},{8,9},{9,8},{10,11... | collective-permute-start | bytes 3145736 | tf_op jit(solution)/shard_map/ppermute | solution.py:79
  6.6 0.0 collective-permute-done.1
  6.6 1.9 %collective-permute-start.2 = (f32[32,2,16,256]{3,2,1,0:T(8,128)}, f32[32,2,16,256]{3,2,1,0:T(8,128)S(1)}, u32[]{:S(2)}, u32[]{:S(2)}) collective-permute-start(f32[32,2,16,256]{3,2,1,0:T(8,128)} %raw.1), channel_id=1, source_target_pairs={{2,0},{5,1},{10,2},{19,3},{12,4},{21,5},{4,6},{3,7},{0,8},{25,9},{... | collective-permute-start | bytes 3145736 | tf_op jit(solution)/shard_map/ppermute | solution.py:328
  8.5 2.4 %collective-permute-start.5 = (f32[2,16,256]{2,1,0:T(8,128)S(1)}, f32[2,16,256]{2,1,0:T(8,128)S(1)}, u32[]{:S(2)}, u32[]{:S(2)}) collective-permute-start(f32[2,16,256]{2,1,0:T(8,128)S(1)} %add.46), channel_id=1, source_target_pairs={{96,0},{98,2},{100,4},{102,6},{104,8},{106,10},{108,12},{110,14},{... | collective-permute-start | bytes 98312 | tf_op jit(solution)/shard_map/ppermute | solution.py:44
  10.9 2.1 %collective-permute-start.4 = (f32[2,16,256]{2,1,0:T(8,128)S(1)}, f32[2,16,256]{2,1,0:T(8,128)S(1)}, u32[]{:S(2)}, u32[]{:S(2)}) collective-permute-start(f32[2,16,256]{2,1,0:T(8,128)S(1)} %add.46), channel_id=1, source_target_pairs={{32,0},{34,2},{36,4},{38,6},{40,8},{42,10},{44,12},{46,14},{48,16}... | collective-permute-start | bytes 98312 | tf_op jit(solution)/shard_map/ppermute | solution.py:44
  13.1 4.5 %collective-permute-start.3 = (f32[2,16,256]{2,1,0:T(8,128)S(1)}, f32[2,16,256]{2,1,0:T(8,128)S(1)}, u32[]{:S(2)}, u32[]{:S(2)}) collective-permute-start(f32[2,16,256]{2,1,0:T(8,128)S(1)} %add.46), channel_id=1, source_target_pairs={{64,0},{66,2},{68,4},{70,6},{72,8},{74,10},{76,12},{78,14},{80,16}... | collective-permute-start | bytes 98312 | tf_op jit(solution)/shard_map/ppermute | solution.py:44
  17.5 0.0 collective-permute-done.5
  17.5 0.0 collective-permute-done.4
  17.5 2.8 %collective-permute-done.3 = f32[2,16,256]{2,1,0:T(8,128)S(1)} collective-permute-done((f32[2,16,256]{2,1,0:T(8,128)S(1)}, f32[2,16,256]{2,1,0:T(8,128)S(1)}, u32[]{:S(2)}, u32[]{:S(2)}) %collective-permute-start.3) | collective-permute-done | bytes 32800 | tf_op jit(solution)/shard_map/ppermute | solution.py:44
  20.3 2.4 %collective-permute-start.8 = (f32[2,16,256]{2,1,0:T(8,128)S(1)}, f32[2,16,256]{2,1,0:T(8,128)S(1)}, u32[]{:S(2)}, u32[]{:S(2)}) collective-permute-start(f32[2,16,256]{2,1,0:T(8,128)S(1)} %add_add_fusion.1), channel_id=1, source_target_pairs={{12,0},{14,2},{0,4},{2,6},{4,8},{6,10},{8,12},{10,14},{28,16},{30,... | collective-permute-start | bytes 98312 | tf_op jit(solution)/shard_map/ppermute | solution.py:44
  22.7 0.3 collective-permute-start.7
  23.1 1.6 %collective-permute-start.6 = (f32[2,16,256]{2,1,0:T(8,128)S(1)}, f32[2,16,256]{2,1,0:T(8,128)S(1)}, u32[]{:S(2)}, u32[]{:S(2)}) collective-permute-start(f32[2,16,256]{2,1,0:T(8,128)S(1)} %add_add_fusion.1), channel_id=1, source_target_pairs={{8,0},{10,2},{12,4},{14,6},{0,8},{2,10},{4,12},{6,14},{24,16},{26,... | collective-permute-start | bytes 98312 | tf_op jit(solution)/shard_map/ppermute | solution.py:44
  24.6 0.0 collective-permute-done.8
  24.7 1.1 %collective-permute-done.7 = f32[2,16,256]{2,1,0:T(8,128)S(1)} collective-permute-done((f32[2,16,256]{2,1,0:T(8,128)S(1)}, f32[2,16,256]{2,1,0:T(8,128)S(1)}, u32[]{:S(2)}, u32[]{:S(2)}) %collective-permute-start.7) | collective-permute-done | bytes 32800 | tf_op jit(solution)/shard_map/ppermute | solution.py:44
  25.8 1.8 %collective-permute-done.6 = f32[2,16,256]{2,1,0:T(8,128)S(1)} collective-permute-done((f32[2,16,256]{2,1,0:T(8,128)S(1)}, f32[2,16,256]{2,1,0:T(8,128)S(1)}, u32[]{:S(2)}, u32[]{:S(2)}) %collective-permute-start.6) | collective-permute-done | bytes 32800 | tf_op jit(solution)/shard_map/ppermute | solution.py:44
  27.6 5.6 %collective-permute-start.9 = (f32[2,16,256]{2,1,0:T(8,128)S(1)}, f32[2,16,256]{2,1,0:T(8,128)S(1)}, u32[]{:S(2)}, u32[]{:S(2)}) collective-permute-start(f32[2,16,256]{2,1,0:T(8,128)S(1)} %add_add_fusion), channel_id=1, source_target_pairs={{2,0},{0,2},{6,4},{4,6},{10,8},{8,10},{14,12},{12,14},{18,16},{16,... | collective-permute-start | bytes 98312 | tf_op jit(solution)/shard_map/ppermute | solution.py:44
  33.2 0.9 %collective-permute-done.9 = f32[2,16,256]{2,1,0:T(8,128)S(1)} collective-permute-done((f32[2,16,256]{2,1,0:T(8,128)S(1)}, f32[2,16,256]{2,1,0:T(8,128)S(1)}, u32[]{:S(2)}, u32[]{:S(2)}) %collective-permute-start.9) | collective-permute-done | bytes 32800 | tf_op jit(solution)/shard_map/ppermute | solution.py:44
  34.1 0.0 collective-permute-done.other
  34.1 0.0 collective-permute-done.2.far0
  34.1 0.4 collective-permute-start.13
  34.5 0.1 add_add_fusion.2
  34.6 8.0 %collective-permute-start.12 = (f32[2,16,256]{2,1,0:T(8,128)S(1)}, f32[2,16,256]{2,1,0:T(8,128)S(1)}, u32[]{:S(2)}, u32[]{:S(2)}) collective-permute-start(f32[2,16,256]{2,1,0:T(8,128)S(1)} %add.53.sum0), channel_id=1, source_target_pairs={{0,129},{1,128},{2,131},{3,130},{4,133},{5,132},{6,135},{7,134},{8... | collective-permute-start | bytes 98312 | tf_op jit(solution)/shard_map/ppermute | solution.py:72
  42.5 0.4 collective-permute-start.11
  42.9 0.3 collective-permute-start.10
  43.2 0.1 add_add_fusion.3.place
  43.3 0.5 collective-permute-done.12.near1
  43.9 3.0 %collective-permute-done.11.sum1 = f32[2,16,256]{2,1,0:T(8,128)S(1)} collective-permute-done((f32[2,16,256]{2,1,0:T(8,128)S(1)}, f32[2,16,256]{2,1,0:T(8,128)S(1)}, u32[]{:S(2)}, u32[]{:S(2)}) %collective-permute-start.11) | collective-permute-done | bytes 32800 | tf_op jit(solution)/shard_map/ppermute | solution.py:79
  46.8 0.0 collective-permute-done.10.near0
  46.8 0.0 copy-start
  46.8 1.2 %copy-done = f32[32,2,16,256]{3,2,1,0:T(8,128)S(1)} copy-done((f32[32,2,16,256]{3,2,1,0:T(8,128)S(1)}, f32[32,2,16,256]{3,2,1,0:T(8,128)}, u32[]{:S(2)}) %copy-start) | copy-done | bytes 1048600
  48.0 0.0 copy-start.1
  48.0 1.1 %copy-done.1 = bf16[2,768,256]{2,1,0:T(8,128)(2,1)S(1)} copy-done((bf16[2,768,256]{2,1,0:T(8,128)(2,1)S(1)}, bf16[2,768,256]{2,1,0:T(8,128)(2,1)}, u32[]{:S(2)}) %copy-start.1) | copy-done | bytes 786456
  49.2 0.0 copy-start.2
  49.2 0.7 copy-done.2
  49.9 1.5 %own.1 = (f32[4,1536,128]{2,1,0:T(8,128)S(1)}, bf16[2,512,256]{2,1,0:T(8,128)(2,1)S(1)}, f32[32,128]{1,0:T(8,128)S(1)}, f32[32,128]{1,0:T(8,128)S(1)}) custom-call(s32[4]{0:T(128)S(1)} %add_add_fusion.3.place, f32[32,2,16,256]{3,2,1,0:T(8,128)S(1)} %copy-done, f32[32,2,16,256]{3,2,1,0:T(8,128)S(1)} %collective-permute-done.other, ...), custom_call_target="tpu_custom_call" | custom-call | tf_op jit(solution)/shard_map/own/pallas_call | solution.py:170
  51.5 0.0 collective-permute-done.13.far1
  51.5 7.5 %edge.2 = (f32[16,16,128]{2,1,0:T(8,128)S(1)}, f32[16,16,128]{2,1,0:T(8,128)S(1)}, f32[16,32,128]{2,1,0:T(8,128)S(1)}) custom-call(s32[4]{0:T(128)S(1)} %get-tuple-element.40.place, f32[4,1536,128]{2,1,0:T(8,128)S(1)} %get-tuple-element.26.a_rows, f32[32,2,16,256]{3,2,1,0:T(8,128)S(1)} %collective-permute-done.2.far0, ...), custom_call_target="tpu_custom_call" | custom-call | flops 1000000 | bytes 10000 | tf_op jit(solution)/shard_map/edge/pallas_call | solution.py:296
  58.9 6.4 %collective-permute-start.15 = (f32[16,32,128]{2,1,0:T(8,128)S(1)}, f32[16,32,128]{2,1,0:T(8,128)S(1)}, u32[]{:S(2)}, u32[]{:S(2)}) collective-permute-start(f32[16,32,128]{2,1,0:T(8,128)S(1)} %get-tuple-element.35), channel_id=1, source_target_pairs={{0,3},{1,4},{2,11},{3,18},{4,13},{5,20},{6,5},{7,2},{8,1},{9,24},{... | collective-permute-start | bytes 786440 | tf_op jit(solution)/shard_map/ppermute | solution.py:324
  65.3 7.5 %edge.3 = (f32[16,32,128]{2,1,0:T(8,128)S(1)}, f32[16,32,128]{2,1,0:T(8,128)S(1)}, f32[16,32,128]{2,1,0:T(8,128)S(1)}) custom-call(s32[4]{0:T(128)S(1)} %get-tuple-element.39.place, f32[4,1536,128]{2,1,0:T(8,128)S(1)} %get-tuple-element.26.a_rows, f32[32,2,16,256]{3,2,1,0:T(8,128)S(1)} %collective-permute-done.2.far0, ...), custom_call_target="tpu_custom_call" | custom-call | flops 1000000 | bytes 10000 | tf_op jit(solution)/shard_map/edge/pallas_call | solution.py:296
  72.8 0.1 collective-permute-start.14
  72.9 0.0 collective-permute-done.15
  72.9 1.2 %collective-permute-start.16 = (f32[16,32,128]{2,1,0:T(8,128)S(1)}, f32[16,32,128]{2,1,0:T(8,128)S(1)}, u32[]{:S(2)}, u32[]{:S(2)}) collective-permute-start(f32[16,32,128]{2,1,0:T(8,128)S(1)} %get-tuple-element.37), channel_id=1, source_target_pairs={{0,2},{1,5},{2,10},{3,19},{4,12},{5,21},{6,4},{7,3},{8,0},{9,25},{... | collective-permute-start | bytes 786440 | tf_op jit(solution)/shard_map/ppermute | solution.py:324
  74.2 8.3 %collective-permute-done.14 = f32[16,32,128]{2,1,0:T(8,128)S(1)} collective-permute-done((f32[16,32,128]{2,1,0:T(8,128)S(1)}, f32[16,32,128]{2,1,0:T(8,128)S(1)}, u32[]{:S(2)}, u32[]{:S(2)}) %collective-permute-start.14) | collective-permute-done | bytes 262176 | tf_op jit(solution)/shard_map/ppermute | solution.py:79
  82.5 0.0 collective-permute-done.16
  82.5 1.2 %select_select_fusion = f32[4,16,32,128]{3,2,1,0:T(8,128)} fusion(f32[16,32,128]{2,1,0:T(8,128)S(1)} %collective-permute-done.15, f32[16,32,128]{2,1,0:T(8,128)S(1)} %collective-permute-done.16, f32[16,32,128]{2,1,0:T(8,128)S(1)} %collective-permute-done.14, f32[16,32,128]{2,1,0:T(8,128)S(1)} %get-tuple-element.33, pred[4]{0:T(512)(128)(4,1)S(1)} %get-tuple-element.41, ...), kind=kLoop, calls=%fused_computation | loop fusion | flops 786432 | bytes 2097160 | tf_op jit(solution)/shard_map/jit(_where)/select_n | solution.py:373
  (5 shorter events, 0.0 us)
Async XLA Ops:
  1.3 5.3 %collective-permute-start.1 = (f32[2,16,256]{2,1,0:T(8,128)S(1)}, f32[2,16,256]{2,1,0:T(8,128)S(1)}, u32[]{:S(2)}, u32[]{:S(2)}) collective-permute-start(f32[2,16,256]{2,1,0:T(8,128)S(1)} %reduce_sum.9), channel_id=1, source_target_pairs={{16,0},{18,2},{20,4},{22,6},{24,8},{26,10},{28,12},{30,14},{0,16},... | collective-permute-start | bytes 98312 | tf_op jit(solution)/shard_map/ppermute | solution.py:44
  3.9 30.2 %collective-permute-start = (f32[32,2,16,256]{3,2,1,0:T(8,128)}, f32[32,2,16,256]{3,2,1,0:T(8,128)S(1)}, u32[]{:S(2)}, u32[]{:S(2)}) collective-permute-start(f32[32,2,16,256]{3,2,1,0:T(8,128)} %raw.1), channel_id=1, source_target_pairs={{0,1},{1,0},{2,3},{3,2},{4,5},{5,4},{6,7},{7,6},{8,9},{9,8},{10,11... | collective-permute-start | bytes 3145736 | tf_op jit(solution)/shard_map/ppermute | solution.py:79
  6.6 27.5 %collective-permute-start.2 = (f32[32,2,16,256]{3,2,1,0:T(8,128)}, f32[32,2,16,256]{3,2,1,0:T(8,128)S(1)}, u32[]{:S(2)}, u32[]{:S(2)}) collective-permute-start(f32[32,2,16,256]{3,2,1,0:T(8,128)} %raw.1), channel_id=1, source_target_pairs={{2,0},{5,1},{10,2},{19,3},{12,4},{21,5},{4,6},{3,7},{0,8},{25,9},{... | collective-permute-start | bytes 3145736 | tf_op jit(solution)/shard_map/ppermute | solution.py:328
  8.5 9.0 %collective-permute-start.5 = (f32[2,16,256]{2,1,0:T(8,128)S(1)}, f32[2,16,256]{2,1,0:T(8,128)S(1)}, u32[]{:S(2)}, u32[]{:S(2)}) collective-permute-start(f32[2,16,256]{2,1,0:T(8,128)S(1)} %add.46), channel_id=1, source_target_pairs={{96,0},{98,2},{100,4},{102,6},{104,8},{106,10},{108,12},{110,14},{... | collective-permute-start | bytes 98312 | tf_op jit(solution)/shard_map/ppermute | solution.py:44
  10.9 6.6 %collective-permute-start.4 = (f32[2,16,256]{2,1,0:T(8,128)S(1)}, f32[2,16,256]{2,1,0:T(8,128)S(1)}, u32[]{:S(2)}, u32[]{:S(2)}) collective-permute-start(f32[2,16,256]{2,1,0:T(8,128)S(1)} %add.46), channel_id=1, source_target_pairs={{32,0},{34,2},{36,4},{38,6},{40,8},{42,10},{44,12},{46,14},{48,16}... | collective-permute-start | bytes 98312 | tf_op jit(solution)/shard_map/ppermute | solution.py:44
  13.1 7.2 %collective-permute-start.3 = (f32[2,16,256]{2,1,0:T(8,128)S(1)}, f32[2,16,256]{2,1,0:T(8,128)S(1)}, u32[]{:S(2)}, u32[]{:S(2)}) collective-permute-start(f32[2,16,256]{2,1,0:T(8,128)S(1)} %add.46), channel_id=1, source_target_pairs={{64,0},{66,2},{68,4},{70,6},{72,8},{74,10},{76,12},{78,14},{80,16}... | collective-permute-start | bytes 98312 | tf_op jit(solution)/shard_map/ppermute | solution.py:44
  20.3 4.3 %collective-permute-start.8 = (f32[2,16,256]{2,1,0:T(8,128)S(1)}, f32[2,16,256]{2,1,0:T(8,128)S(1)}, u32[]{:S(2)}, u32[]{:S(2)}) collective-permute-start(f32[2,16,256]{2,1,0:T(8,128)S(1)} %add_add_fusion.1), channel_id=1, source_target_pairs={{12,0},{14,2},{0,4},{2,6},{4,8},{6,10},{8,12},{10,14},{28,16},{30,... | collective-permute-start | bytes 98312 | tf_op jit(solution)/shard_map/ppermute | solution.py:44
  22.7 3.1 %collective-permute-start.7 = (f32[2,16,256]{2,1,0:T(8,128)S(1)}, f32[2,16,256]{2,1,0:T(8,128)S(1)}, u32[]{:S(2)}, u32[]{:S(2)}) collective-permute-start(f32[2,16,256]{2,1,0:T(8,128)S(1)} %add_add_fusion.1), channel_id=1, source_target_pairs={{4,0},{6,2},{8,4},{10,6},{12,8},{14,10},{0,12},{2,14},{20,16},{22,... | collective-permute-start | bytes 98312 | tf_op jit(solution)/shard_map/ppermute | solution.py:44
  23.1 4.6 %collective-permute-start.6 = (f32[2,16,256]{2,1,0:T(8,128)S(1)}, f32[2,16,256]{2,1,0:T(8,128)S(1)}, u32[]{:S(2)}, u32[]{:S(2)}) collective-permute-start(f32[2,16,256]{2,1,0:T(8,128)S(1)} %add_add_fusion.1), channel_id=1, source_target_pairs={{8,0},{10,2},{12,4},{14,6},{0,8},{2,10},{4,12},{6,14},{24,16},{26,... | collective-permute-start | bytes 98312 | tf_op jit(solution)/shard_map/ppermute | solution.py:44
  27.6 6.4 %collective-permute-start.9 = (f32[2,16,256]{2,1,0:T(8,128)S(1)}, f32[2,16,256]{2,1,0:T(8,128)S(1)}, u32[]{:S(2)}, u32[]{:S(2)}) collective-permute-start(f32[2,16,256]{2,1,0:T(8,128)S(1)} %add_add_fusion), channel_id=1, source_target_pairs={{2,0},{0,2},{6,4},{4,6},{10,8},{8,10},{14,12},{12,14},{18,16},{16,... | collective-permute-start | bytes 98312 | tf_op jit(solution)/shard_map/ppermute | solution.py:44
  34.1 17.4 %collective-permute-start.13 = (f32[32,2,16,256]{3,2,1,0:T(8,128)S(1)}, f32[32,2,16,256]{3,2,1,0:T(8,128)S(1)}, u32[]{:S(2)}, u32[]{:S(2)}) collective-permute-start(f32[32,2,16,256]{3,2,1,0:T(8,128)S(1)} %collective-permute-done.other), channel_id=1, source_target_pairs={{2,0},{5,1},{10,2},{19,3},{12,4},{21,5},{4,6},{3,7},{0,8},{25,9},{... | collective-permute-start | bytes 3145736 | tf_op jit(solution)/shard_map/ppermute | solution.py:328
  34.6 9.3 %collective-permute-start.12 = (f32[2,16,256]{2,1,0:T(8,128)S(1)}, f32[2,16,256]{2,1,0:T(8,128)S(1)}, u32[]{:S(2)}, u32[]{:S(2)}) collective-permute-start(f32[2,16,256]{2,1,0:T(8,128)S(1)} %add.53.sum0), channel_id=1, source_target_pairs={{0,129},{1,128},{2,131},{3,130},{4,133},{5,132},{6,135},{7,134},{8... | collective-permute-start | bytes 98312 | tf_op jit(solution)/shard_map/ppermute | solution.py:72
  42.5 4.3 %collective-permute-start.11 = (f32[2,16,256]{2,1,0:T(8,128)S(1)}, f32[2,16,256]{2,1,0:T(8,128)S(1)}, u32[]{:S(2)}, u32[]{:S(2)}) collective-permute-start(f32[2,16,256]{2,1,0:T(8,128)S(1)} %add.53.sum0), channel_id=1, source_target_pairs={{0,1},{1,0},{2,3},{3,2},{4,5},{5,4},{6,7},{7,6},{8,9},{9,8},{10,11... | collective-permute-start | bytes 98312 | tf_op jit(solution)/shard_map/ppermute | solution.py:79
  42.9 3.9 %collective-permute-start.10 = (f32[2,16,256]{2,1,0:T(8,128)S(1)}, f32[2,16,256]{2,1,0:T(8,128)S(1)}, u32[]{:S(2)}, u32[]{:S(2)}) collective-permute-start(f32[2,16,256]{2,1,0:T(8,128)S(1)} %add.53.sum0), channel_id=1, source_target_pairs={{128,0},{130,2},{132,4},{134,6},{136,8},{138,10},{140,12},{142,14}... | collective-permute-start | bytes 98312 | tf_op jit(solution)/shard_map/ppermute | solution.py:44
  46.8 1.2 %copy-start = (f32[32,2,16,256]{3,2,1,0:T(8,128)S(1)}, f32[32,2,16,256]{3,2,1,0:T(8,128)}, u32[]{:S(2)}) copy-start(f32[32,2,16,256]{3,2,1,0:T(8,128)} %raw.1) | copy-start | bytes 3145732
  48.0 1.1 %copy-start.1 = (bf16[2,768,256]{2,1,0:T(8,128)(2,1)S(1)}, bf16[2,768,256]{2,1,0:T(8,128)(2,1)}, u32[]{:S(2)}) copy-start(bf16[2,768,256]{2,1,0:T(8,128)(2,1)} %constant.48.clone.all_tables) | copy-start | bytes 2359300
  49.2 0.7 copy-start.2
  58.9 14.0 %collective-permute-start.15 = (f32[16,32,128]{2,1,0:T(8,128)S(1)}, f32[16,32,128]{2,1,0:T(8,128)S(1)}, u32[]{:S(2)}, u32[]{:S(2)}) collective-permute-start(f32[16,32,128]{2,1,0:T(8,128)S(1)} %get-tuple-element.35), channel_id=1, source_target_pairs={{0,3},{1,4},{2,11},{3,18},{4,13},{5,20},{6,5},{7,2},{8,1},{9,24},{... | collective-permute-start | bytes 786440 | tf_op jit(solution)/shard_map/ppermute | solution.py:324
  72.8 9.7 %collective-permute-start.14 = (f32[16,32,128]{2,1,0:T(8,128)S(1)}, f32[16,32,128]{2,1,0:T(8,128)S(1)}, u32[]{:S(2)}, u32[]{:S(2)}) collective-permute-start(f32[16,32,128]{2,1,0:T(8,128)S(1)} %get-tuple-element.34), channel_id=1, source_target_pairs={{0,1},{1,0},{2,3},{3,2},{4,5},{5,4},{6,7},{7,6},{8,9},{9,8},{10,11... | collective-permute-start | bytes 786440 | tf_op jit(solution)/shard_map/ppermute | solution.py:79
  72.9 9.6 %collective-permute-start.16 = (f32[16,32,128]{2,1,0:T(8,128)S(1)}, f32[16,32,128]{2,1,0:T(8,128)S(1)}, u32[]{:S(2)}, u32[]{:S(2)}) collective-permute-start(f32[16,32,128]{2,1,0:T(8,128)S(1)} %get-tuple-element.37), channel_id=1, source_target_pairs={{0,2},{1,5},{2,10},{3,19},{4,12},{5,21},{6,4},{7,3},{8,0},{9,25},{... | collective-permute-start | bytes 786440 | tf_op jit(solution)/shard_map/ppermute | solution.py:324

commit v3 on v2

--- a/solution.py
+++ b/solution.py
@@ -242,7 +242,7 @@
 
     lax.fori_loop(0, chans // A_TILE, products, 0)
     far_counts = far_n[pl.ds(b0, hrows), :]
-    group = 8
+    group = 16
 
     def lagged(t, carry):
         size = group * hrows

time: 84 us -> 83.5 us (level)
  no operation moved by 1% of the time
where the time goes in v3:
time: 83.5 us; the launch traced here: 83.2 us
  starting transfers between devices  42.9 us (51%)
  waiting for transfers between devices  18.5 us (22%)
  Pallas kernels  16 us (19%)
  local copies, waits for them, and re-layouts  3.08 us (4%)
  other arithmetic  2.7 us (3%)
    ppermute x9, starting transfers between devices, from_chan(): lax.ppermute(block, 'chan', [(source(i), i) for i in range(chan_count)])  21.7 us
    pallas_call x2, Pallas kernels, edge(): pl.pallas_call(functools.partial(edge_body, not before), out_shape=(mine,...  14.4 us
    ppermute x3, waiting for transfers between devices, swap_freq(): return lax.ppermute(block, 'freq', [(0, 1), (1, 0)])  11.3 us
    ppermute x1, starting transfers between devices, sum_over_chan(): lax.ppermute(sums, ('chan', 'freq'), [(d, d ^ 2 * top ^ 1) for d in range...  7.96 us
    ppermute x2, starting transfers between devices, to_partner(): return lax.ppermute(block, ('chan', 'freq'), edge_route(size, flip))  7.63 us
    ppermute x9, waiting for transfers between devices, from_chan(): lax.ppermute(block, 'chan', [(source(i), i) for i in range(chan_count)])  6.65 us
    ppermute x3, starting transfers between devices, swap_freq(): return lax.ppermute(block, 'freq', [(0, 1), (1, 0)])  3.2 us
    unnamed x6, local copies, waits for them, and re-layouts  3.08 us
  transfers between devices with their start and end apart: 17, of which 7 were waited for; matrix products, arithmetic and copies ran while one was open for 0% of the time, Pallas kernels for 11%

profile of v3, /device:TPU:1, one launch (start us, length us, event | category | flops | bytes accessed | tf_op | source)
XLA Modules:
  0.0 83.2 jit_solution(11964597810215420893)
XLA Ops:
  0.0 1.3 %reduce_sum.9 = f32[2,16,256]{2,1,0:T(8,128)S(1)} reduce(f32[32,2,16,256]{3,2,1,0:T(8,128)} %raw.1, f32[]{:T(128)} %constant.47.clone.1), dimensions={0}, to_apply=%region_0.0 | reduce | flops 253952 | bytes 1081348 | tf_op jit(solution)/shard_map/reduce_sum | solution.py:334
  1.3 2.6 %collective-permute-start.1 = (f32[2,16,256]{2,1,0:T(8,128)S(1)}, f32[2,16,256]{2,1,0:T(8,128)S(1)}, u32[]{:S(2)}, u32[]{:S(2)}) collective-permute-start(f32[2,16,256]{2,1,0:T(8,128)S(1)} %reduce_sum.9), channel_id=1, source_target_pairs={{16,0},{18,2},{20,4},{22,6},{24,8},{26,10},{28,12},{30,14},{0,16},... | collective-permute-start | bytes 98312 | tf_op jit(solution)/shard_map/ppermute | solution.py:44
  3.9 2.7 %collective-permute-start = (f32[32,2,16,256]{3,2,1,0:T(8,128)}, f32[32,2,16,256]{3,2,1,0:T(8,128)S(1)}, u32[]{:S(2)}, u32[]{:S(2)}) collective-permute-start(f32[32,2,16,256]{3,2,1,0:T(8,128)} %raw.1), channel_id=1, source_target_pairs={{0,1},{1,0},{2,3},{3,2},{4,5},{5,4},{6,7},{7,6},{8,9},{9,8},{10,11... | collective-permute-start | bytes 3145736 | tf_op jit(solution)/shard_map/ppermute | solution.py:79
  6.6 0.0 collective-permute-done.1
  6.6 1.9 %collective-permute-start.2 = (f32[32,2,16,256]{3,2,1,0:T(8,128)}, f32[32,2,16,256]{3,2,1,0:T(8,128)S(1)}, u32[]{:S(2)}, u32[]{:S(2)}) collective-permute-start(f32[32,2,16,256]{3,2,1,0:T(8,128)} %raw.1), channel_id=1, source_target_pairs={{2,0},{5,1},{10,2},{19,3},{12,4},{21,5},{4,6},{3,7},{0,8},{25,9},{... | collective-permute-start | bytes 3145736 | tf_op jit(solution)/shard_map/ppermute | solution.py:328
  8.5 2.4 %collective-permute-start.5 = (f32[2,16,256]{2,1,0:T(8,128)S(1)}, f32[2,16,256]{2,1,0:T(8,128)S(1)}, u32[]{:S(2)}, u32[]{:S(2)}) collective-permute-start(f32[2,16,256]{2,1,0:T(8,128)S(1)} %add.46), channel_id=1, source_target_pairs={{96,0},{98,2},{100,4},{102,6},{104,8},{106,10},{108,12},{110,14},{... | collective-permute-start | bytes 98312 | tf_op jit(solution)/shard_map/ppermute | solution.py:44
  10.9 2.1 %collective-permute-start.4 = (f32[2,16,256]{2,1,0:T(8,128)S(1)}, f32[2,16,256]{2,1,0:T(8,128)S(1)}, u32[]{:S(2)}, u32[]{:S(2)}) collective-permute-start(f32[2,16,256]{2,1,0:T(8,128)S(1)} %add.46), channel_id=1, source_target_pairs={{32,0},{34,2},{36,4},{38,6},{40,8},{42,10},{44,12},{46,14},{48,16}... | collective-permute-start | bytes 98312 | tf_op jit(solution)/shard_map/ppermute | solution.py:44
  13.1 4.5 %collective-permute-start.3 = (f32[2,16,256]{2,1,0:T(8,128)S(1)}, f32[2,16,256]{2,1,0:T(8,128)S(1)}, u32[]{:S(2)}, u32[]{:S(2)}) collective-permute-start(f32[2,16,256]{2,1,0:T(8,128)S(1)} %add.46), channel_id=1, source_target_pairs={{64,0},{66,2},{68,4},{70,6},{72,8},{74,10},{76,12},{78,14},{80,16}... | collective-permute-start | bytes 98312 | tf_op jit(solution)/shard_map/ppermute | solution.py:44
  17.5 0.0 collective-permute-done.5
  17.5 0.0 collective-permute-done.4
  17.5 2.8 %collective-permute-done.3 = f32[2,16,256]{2,1,0:T(8,128)S(1)} collective-permute-done((f32[2,16,256]{2,1,0:T(8,128)S(1)}, f32[2,16,256]{2,1,0:T(8,128)S(1)}, u32[]{:S(2)}, u32[]{:S(2)}) %collective-permute-start.3) | collective-permute-done | bytes 32800 | tf_op jit(solution)/shard_map/ppermute | solution.py:44
  20.3 2.4 %collective-permute-start.8 = (f32[2,16,256]{2,1,0:T(8,128)S(1)}, f32[2,16,256]{2,1,0:T(8,128)S(1)}, u32[]{:S(2)}, u32[]{:S(2)}) collective-permute-start(f32[2,16,256]{2,1,0:T(8,128)S(1)} %add_add_fusion.1), channel_id=1, source_target_pairs={{12,0},{14,2},{0,4},{2,6},{4,8},{6,10},{8,12},{10,14},{28,16},{30,... | collective-permute-start | bytes 98312 | tf_op jit(solution)/shard_map/ppermute | solution.py:44
  22.7 0.3 collective-permute-start.7
  23.1 1.6 %collective-permute-start.6 = (f32[2,16,256]{2,1,0:T(8,128)S(1)}, f32[2,16,256]{2,1,0:T(8,128)S(1)}, u32[]{:S(2)}, u32[]{:S(2)}) collective-permute-start(f32[2,16,256]{2,1,0:T(8,128)S(1)} %add_add_fusion.1), channel_id=1, source_target_pairs={{8,0},{10,2},{12,4},{14,6},{0,8},{2,10},{4,12},{6,14},{24,16},{26,... | collective-permute-start | bytes 98312 | tf_op jit(solution)/shard_map/ppermute | solution.py:44
  24.6 0.0 collective-permute-done.8
  24.7 1.1 %collective-permute-done.7 = f32[2,16,256]{2,1,0:T(8,128)S(1)} collective-permute-done((f32[2,16,256]{2,1,0:T(8,128)S(1)}, f32[2,16,256]{2,1,0:T(8,128)S(1)}, u32[]{:S(2)}, u32[]{:S(2)}) %collective-permute-start.7) | collective-permute-done | bytes 32800 | tf_op jit(solution)/shard_map/ppermute | solution.py:44
  25.8 1.8 %collective-permute-done.6 = f32[2,16,256]{2,1,0:T(8,128)S(1)} collective-permute-done((f32[2,16,256]{2,1,0:T(8,128)S(1)}, f32[2,16,256]{2,1,0:T(8,128)S(1)}, u32[]{:S(2)}, u32[]{:S(2)}) %collective-permute-start.6) | collective-permute-done | bytes 32800 | tf_op jit(solution)/shard_map/ppermute | solution.py:44
  27.6 5.6 %collective-permute-start.9 = (f32[2,16,256]{2,1,0:T(8,128)S(1)}, f32[2,16,256]{2,1,0:T(8,128)S(1)}, u32[]{:S(2)}, u32[]{:S(2)}) collective-permute-start(f32[2,16,256]{2,1,0:T(8,128)S(1)} %add_add_fusion), channel_id=1, source_target_pairs={{2,0},{0,2},{6,4},{4,6},{10,8},{8,10},{14,12},{12,14},{18,16},{16,... | collective-permute-start | bytes 98312 | tf_op jit(solution)/shard_map/ppermute | solution.py:44
  33.2 0.9 %collective-permute-done.9 = f32[2,16,256]{2,1,0:T(8,128)S(1)} collective-permute-done((f32[2,16,256]{2,1,0:T(8,128)S(1)}, f32[2,16,256]{2,1,0:T(8,128)S(1)}, u32[]{:S(2)}, u32[]{:S(2)}) %collective-permute-start.9) | collective-permute-done | bytes 32800 | tf_op jit(solution)/shard_map/ppermute | solution.py:44
  34.1 0.0 collective-permute-done.other
  34.1 0.0 collective-permute-done.2.far0
  34.1 0.4 collective-permute-start.13
  34.5 0.1 add_add_fusion.2
  34.6 8.0 %collective-permute-start.12 = (f32[2,16,256]{2,1,0:T(8,128)S(1)}, f32[2,16,256]{2,1,0:T(8,128)S(1)}, u32[]{:S(2)}, u32[]{:S(2)}) collective-permute-start(f32[2,16,256]{2,1,0:T(8,128)S(1)} %add.53.sum0), channel_id=1, source_target_pairs={{0,129},{1,128},{2,131},{3,130},{4,133},{5,132},{6,135},{7,134},{8... | collective-permute-start | bytes 98312 | tf_op jit(solution)/shard_map/ppermute | solution.py:72
  42.5 0.4 collective-permute-start.11
  42.9 0.3 collective-permute-start.10
  43.2 0.1 add_add_fusion.3.place
  43.3 0.5 collective-permute-done.12.near1
  43.9 3.0 %collective-permute-done.11.sum1 = f32[2,16,256]{2,1,0:T(8,128)S(1)} collective-permute-done((f32[2,16,256]{2,1,0:T(8,128)S(1)}, f32[2,16,256]{2,1,0:T(8,128)S(1)}, u32[]{:S(2)}, u32[]{:S(2)}) %collective-permute-start.11) | collective-permute-done | bytes 32800 | tf_op jit(solution)/shard_map/ppermute | solution.py:79
  46.8 0.0 collective-permute-done.10.near0
  46.8 0.0 copy-start
  46.8 1.2 %copy-done = f32[32,2,16,256]{3,2,1,0:T(8,128)S(1)} copy-done((f32[32,2,16,256]{3,2,1,0:T(8,128)S(1)}, f32[32,2,16,256]{3,2,1,0:T(8,128)}, u32[]{:S(2)}) %copy-start) | copy-done | bytes 1048600
  48.0 0.0 copy-start.1
  48.0 1.1 %copy-done.1 = bf16[2,768,256]{2,1,0:T(8,128)(2,1)S(1)} copy-done((bf16[2,768,256]{2,1,0:T(8,128)(2,1)S(1)}, bf16[2,768,256]{2,1,0:T(8,128)(2,1)}, u32[]{:S(2)}) %copy-start.1) | copy-done | bytes 786456
  49.2 0.0 copy-start.2
  49.2 0.7 copy-done.2
  49.9 1.5 %own.1 = (f32[4,1536,128]{2,1,0:T(8,128)S(1)}, bf16[2,512,256]{2,1,0:T(8,128)(2,1)S(1)}, f32[32,128]{1,0:T(8,128)S(1)}, f32[32,128]{1,0:T(8,128)S(1)}) custom-call(s32[4]{0:T(128)S(1)} %add_add_fusion.3.place, f32[32,2,16,256]{3,2,1,0:T(8,128)S(1)} %copy-done, f32[32,2,16,256]{3,2,1,0:T(8,128)S(1)} %collective-permute-done.other, ...), custom_call_target="tpu_custom_call" | custom-call | tf_op jit(solution)/shard_map/own/pallas_call | solution.py:170
  51.5 0.0 collective-permute-done.13.far1
  51.5 7.2 %edge.2 = (f32[16,16,128]{2,1,0:T(8,128)S(1)}, f32[16,16,128]{2,1,0:T(8,128)S(1)}, f32[16,32,128]{2,1,0:T(8,128)S(1)}) custom-call(s32[4]{0:T(128)S(1)} %get-tuple-element.40.place, f32[4,1536,128]{2,1,0:T(8,128)S(1)} %get-tuple-element.26.a_rows, f32[32,2,16,256]{3,2,1,0:T(8,128)S(1)} %collective-permute-done.2.far0, ...), custom_call_target="tpu_custom_call" | custom-call | flops 1000000 | bytes 10000 | tf_op jit(solution)/shard_map/edge/pallas_call | solution.py:296
  58.7 6.4 %collective-permute-start.15 = (f32[16,32,128]{2,1,0:T(8,128)S(1)}, f32[16,32,128]{2,1,0:T(8,128)S(1)}, u32[]{:S(2)}, u32[]{:S(2)}) collective-permute-start(f32[16,32,128]{2,1,0:T(8,128)S(1)} %get-tuple-element.35), channel_id=1, source_target_pairs={{0,3},{1,4},{2,11},{3,18},{4,13},{5,20},{6,5},{7,2},{8,1},{9,24},{... | collective-permute-start | bytes 786440 | tf_op jit(solution)/shard_map/ppermute | solution.py:324
  65.1 7.2 %edge.3 = (f32[16,32,128]{2,1,0:T(8,128)S(1)}, f32[16,32,128]{2,1,0:T(8,128)S(1)}, f32[16,32,128]{2,1,0:T(8,128)S(1)}) custom-call(s32[4]{0:T(128)S(1)} %get-tuple-element.39.place, f32[4,1536,128]{2,1,0:T(8,128)S(1)} %get-tuple-element.26.a_rows, f32[32,2,16,256]{3,2,1,0:T(8,128)S(1)} %collective-permute-done.2.far0, ...), custom_call_target="tpu_custom_call" | custom-call | flops 1000000 | bytes 10000 | tf_op jit(solution)/shard_map/edge/pallas_call | solution.py:296
  72.3 0.1 collective-permute-start.14
  72.4 0.0 collective-permute-done.15
  72.4 1.2 %collective-permute-start.16 = (f32[16,32,128]{2,1,0:T(8,128)S(1)}, f32[16,32,128]{2,1,0:T(8,128)S(1)}, u32[]{:S(2)}, u32[]{:S(2)}) collective-permute-start(f32[16,32,128]{2,1,0:T(8,128)S(1)} %get-tuple-element.37), channel_id=1, source_target_pairs={{0,2},{1,5},{2,10},{3,19},{4,12},{5,21},{6,4},{7,3},{8,0},{9,25},{... | collective-permute-start | bytes 786440 | tf_op jit(solution)/shard_map/ppermute | solution.py:324
  73.7 8.3 %collective-permute-done.14 = f32[16,32,128]{2,1,0:T(8,128)S(1)} collective-permute-done((f32[16,32,128]{2,1,0:T(8,128)S(1)}, f32[16,32,128]{2,1,0:T(8,128)S(1)}, u32[]{:S(2)}, u32[]{:S(2)}) %collective-permute-start.14) | collective-permute-done | bytes 262176 | tf_op jit(solution)/shard_map/ppermute | solution.py:79
  82.0 0.0 collective-permute-done.16
  82.0 1.2 %select_select_fusion = f32[4,16,32,128]{3,2,1,0:T(8,128)} fusion(f32[16,32,128]{2,1,0:T(8,128)S(1)} %collective-permute-done.15, f32[16,32,128]{2,1,0:T(8,128)S(1)} %collective-permute-done.16, f32[16,32,128]{2,1,0:T(8,128)S(1)} %collective-permute-done.14, f32[16,32,128]{2,1,0:T(8,128)S(1)} %get-tuple-element.33, pred[4]{0:T(512)(128)(4,1)S(1)} %get-tuple-element.41, ...), kind=kLoop, calls=%fused_computation | loop fusion | flops 786432 | bytes 2097160 | tf_op jit(solution)/shard_map/jit(_where)/select_n | solution.py:373
  (5 shorter events, 0.0 us)
Async XLA Ops:
  1.3 5.3 %collective-permute-start.1 = (f32[2,16,256]{2,1,0:T(8,128)S(1)}, f32[2,16,256]{2,1,0:T(8,128)S(1)}, u32[]{:S(2)}, u32[]{:S(2)}) collective-permute-start(f32[2,16,256]{2,1,0:T(8,128)S(1)} %reduce_sum.9), channel_id=1, source_target_pairs={{16,0},{18,2},{20,4},{22,6},{24,8},{26,10},{28,12},{30,14},{0,16},... | collective-permute-start | bytes 98312 | tf_op jit(solution)/shard_map/ppermute | solution.py:44
  3.9 30.2 %collective-permute-start = (f32[32,2,16,256]{3,2,1,0:T(8,128)}, f32[32,2,16,256]{3,2,1,0:T(8,128)S(1)}, u32[]{:S(2)}, u32[]{:S(2)}) collective-permute-start(f32[32,2,16,256]{3,2,1,0:T(8,128)} %raw.1), channel_id=1, source_target_pairs={{0,1},{1,0},{2,3},{3,2},{4,5},{5,4},{6,7},{7,6},{8,9},{9,8},{10,11... | collective-permute-start | bytes 3145736 | tf_op jit(solution)/shard_map/ppermute | solution.py:79
  6.6 27.5 %collective-permute-start.2 = (f32[32,2,16,256]{3,2,1,0:T(8,128)}, f32[32,2,16,256]{3,2,1,0:T(8,128)S(1)}, u32[]{:S(2)}, u32[]{:S(2)}) collective-permute-start(f32[32,2,16,256]{3,2,1,0:T(8,128)} %raw.1), channel_id=1, source_target_pairs={{2,0},{5,1},{10,2},{19,3},{12,4},{21,5},{4,6},{3,7},{0,8},{25,9},{... | collective-permute-start | bytes 3145736 | tf_op jit(solution)/shard_map/ppermute | solution.py:328
  8.5 9.0 %collective-permute-start.5 = (f32[2,16,256]{2,1,0:T(8,128)S(1)}, f32[2,16,256]{2,1,0:T(8,128)S(1)}, u32[]{:S(2)}, u32[]{:S(2)}) collective-permute-start(f32[2,16,256]{2,1,0:T(8,128)S(1)} %add.46), channel_id=1, source_target_pairs={{96,0},{98,2},{100,4},{102,6},{104,8},{106,10},{108,12},{110,14},{... | collective-permute-start | bytes 98312 | tf_op jit(solution)/shard_map/ppermute | solution.py:44
  10.9 6.6 %collective-permute-start.4 = (f32[2,16,256]{2,1,0:T(8,128)S(1)}, f32[2,16,256]{2,1,0:T(8,128)S(1)}, u32[]{:S(2)}, u32[]{:S(2)}) collective-permute-start(f32[2,16,256]{2,1,0:T(8,128)S(1)} %add.46), channel_id=1, source_target_pairs={{32,0},{34,2},{36,4},{38,6},{40,8},{42,10},{44,12},{46,14},{48,16}... | collective-permute-start | bytes 98312 | tf_op jit(solution)/shard_map/ppermute | solution.py:44
  13.1 7.2 %collective-permute-start.3 = (f32[2,16,256]{2,1,0:T(8,128)S(1)}, f32[2,16,256]{2,1,0:T(8,128)S(1)}, u32[]{:S(2)}, u32[]{:S(2)}) collective-permute-start(f32[2,16,256]{2,1,0:T(8,128)S(1)} %add.46), channel_id=1, source_target_pairs={{64,0},{66,2},{68,4},{70,6},{72,8},{74,10},{76,12},{78,14},{80,16}... | collective-permute-start | bytes 98312 | tf_op jit(solution)/shard_map/ppermute | solution.py:44
  20.3 4.3 %collective-permute-start.8 = (f32[2,16,256]{2,1,0:T(8,128)S(1)}, f32[2,16,256]{2,1,0:T(8,128)S(1)}, u32[]{:S(2)}, u32[]{:S(2)}) collective-permute-start(f32[2,16,256]{2,1,0:T(8,128)S(1)} %add_add_fusion.1), channel_id=1, source_target_pairs={{12,0},{14,2},{0,4},{2,6},{4,8},{6,10},{8,12},{10,14},{28,16},{30,... | collective-permute-start | bytes 98312 | tf_op jit(solution)/shard_map/ppermute | solution.py:44
  22.7 3.1 %collective-permute-start.7 = (f32[2,16,256]{2,1,0:T(8,128)S(1)}, f32[2,16,256]{2,1,0:T(8,128)S(1)}, u32[]{:S(2)}, u32[]{:S(2)}) collective-permute-start(f32[2,16,256]{2,1,0:T(8,128)S(1)} %add_add_fusion.1), channel_id=1, source_target_pairs={{4,0},{6,2},{8,4},{10,6},{12,8},{14,10},{0,12},{2,14},{20,16},{22,... | collective-permute-start | bytes 98312 | tf_op jit(solution)/shard_map/ppermute | solution.py:44
  23.1 4.6 %collective-permute-start.6 = (f32[2,16,256]{2,1,0:T(8,128)S(1)}, f32[2,16,256]{2,1,0:T(8,128)S(1)}, u32[]{:S(2)}, u32[]{:S(2)}) collective-permute-start(f32[2,16,256]{2,1,0:T(8,128)S(1)} %add_add_fusion.1), channel_id=1, source_target_pairs={{8,0},{10,2},{12,4},{14,6},{0,8},{2,10},{4,12},{6,14},{24,16},{26,... | collective-permute-start | bytes 98312 | tf_op jit(solution)/shard_map/ppermute | solution.py:44
  27.6 6.4 %collective-permute-start.9 = (f32[2,16,256]{2,1,0:T(8,128)S(1)}, f32[2,16,256]{2,1,0:T(8,128)S(1)}, u32[]{:S(2)}, u32[]{:S(2)}) collective-permute-start(f32[2,16,256]{2,1,0:T(8,128)S(1)} %add_add_fusion), channel_id=1, source_target_pairs={{2,0},{0,2},{6,4},{4,6},{10,8},{8,10},{14,12},{12,14},{18,16},{16,... | collective-permute-start | bytes 98312 | tf_op jit(solution)/shard_map/ppermute | solution.py:44
  34.1 17.4 %collective-permute-start.13 = (f32[32,2,16,256]{3,2,1,0:T(8,128)S(1)}, f32[32,2,16,256]{3,2,1,0:T(8,128)S(1)}, u32[]{:S(2)}, u32[]{:S(2)}) collective-permute-start(f32[32,2,16,256]{3,2,1,0:T(8,128)S(1)} %collective-permute-done.other), channel_id=1, source_target_pairs={{2,0},{5,1},{10,2},{19,3},{12,4},{21,5},{4,6},{3,7},{0,8},{25,9},{... | collective-permute-start | bytes 3145736 | tf_op jit(solution)/shard_map/ppermute | solution.py:328
  34.6 9.3 %collective-permute-start.12 = (f32[2,16,256]{2,1,0:T(8,128)S(1)}, f32[2,16,256]{2,1,0:T(8,128)S(1)}, u32[]{:S(2)}, u32[]{:S(2)}) collective-permute-start(f32[2,16,256]{2,1,0:T(8,128)S(1)} %add.53.sum0), channel_id=1, source_target_pairs={{0,129},{1,128},{2,131},{3,130},{4,133},{5,132},{6,135},{7,134},{8... | collective-permute-start | bytes 98312 | tf_op jit(solution)/shard_map/ppermute | solution.py:72
  42.5 4.3 %collective-permute-start.11 = (f32[2,16,256]{2,1,0:T(8,128)S(1)}, f32[2,16,256]{2,1,0:T(8,128)S(1)}, u32[]{:S(2)}, u32[]{:S(2)}) collective-permute-start(f32[2,16,256]{2,1,0:T(8,128)S(1)} %add.53.sum0), channel_id=1, source_target_pairs={{0,1},{1,0},{2,3},{3,2},{4,5},{5,4},{6,7},{7,6},{8,9},{9,8},{10,11... | collective-permute-start | bytes 98312 | tf_op jit(solution)/shard_map/ppermute | solution.py:79
  42.9 3.9 %collective-permute-start.10 = (f32[2,16,256]{2,1,0:T(8,128)S(1)}, f32[2,16,256]{2,1,0:T(8,128)S(1)}, u32[]{:S(2)}, u32[]{:S(2)}) collective-permute-start(f32[2,16,256]{2,1,0:T(8,128)S(1)} %add.53.sum0), channel_id=1, source_target_pairs={{128,0},{130,2},{132,4},{134,6},{136,8},{138,10},{140,12},{142,14}... | collective-permute-start | bytes 98312 | tf_op jit(solution)/shard_map/ppermute | solution.py:44
  46.8 1.2 %copy-start = (f32[32,2,16,256]{3,2,1,0:T(8,128)S(1)}, f32[32,2,16,256]{3,2,1,0:T(8,128)}, u32[]{:S(2)}) copy-start(f32[32,2,16,256]{3,2,1,0:T(8,128)} %raw.1) | copy-start | bytes 3145732
  48.0 1.1 %copy-start.1 = (bf16[2,768,256]{2,1,0:T(8,128)(2,1)S(1)}, bf16[2,768,256]{2,1,0:T(8,128)(2,1)}, u32[]{:S(2)}) copy-start(bf16[2,768,256]{2,1,0:T(8,128)(2,1)} %constant.48.clone.all_tables) | copy-start | bytes 2359300
  49.2 0.7 copy-start.2
  58.7 13.7 %collective-permute-start.15 = (f32[16,32,128]{2,1,0:T(8,128)S(1)}, f32[16,32,128]{2,1,0:T(8,128)S(1)}, u32[]{:S(2)}, u32[]{:S(2)}) collective-permute-start(f32[16,32,128]{2,1,0:T(8,128)S(1)} %get-tuple-element.35), channel_id=1, source_target_pairs={{0,3},{1,4},{2,11},{3,18},{4,13},{5,20},{6,5},{7,2},{8,1},{9,24},{... | collective-permute-start | bytes 786440 | tf_op jit(solution)/shard_map/ppermute | solution.py:324
  72.3 9.7 %collective-permute-start.14 = (f32[16,32,128]{2,1,0:T(8,128)S(1)}, f32[16,32,128]{2,1,0:T(8,128)S(1)}, u32[]{:S(2)}, u32[]{:S(2)}) collective-permute-start(f32[16,32,128]{2,1,0:T(8,128)S(1)} %get-tuple-element.34), channel_id=1, source_target_pairs={{0,1},{1,0},{2,3},{3,2},{4,5},{5,4},{6,7},{7,6},{8,9},{9,8},{10,11... | collective-permute-start | bytes 786440 | tf_op jit(solution)/shard_map/ppermute | solution.py:79
  72.4 9.6 %collective-permute-start.16 = (f32[16,32,128]{2,1,0:T(8,128)S(1)}, f32[16,32,128]{2,1,0:T(8,128)S(1)}, u32[]{:S(2)}, u32[]{:S(2)}) collective-permute-start(f32[16,32,128]{2,1,0:T(8,128)S(1)} %get-tuple-element.37), channel_id=1, source_target_pairs={{0,2},{1,5},{2,10},{3,19},{4,12},{5,21},{6,4},{7,3},{8,0},{9,25},{... | collective-permute-start | bytes 786440 | tf_op jit(solution)/shard_map/ppermute | solution.py:324

commit v4 on v3

--- a/solution.py
+++ b/solution.py
@@ -242,7 +242,7 @@
 
     lax.fori_loop(0, chans // A_TILE, products, 0)
     far_counts = far_n[pl.ds(b0, hrows), :]
-    group = 16
+    group = 32
 
     def lagged(t, carry):
         size = group * hrows

time: 83.5 us -> 83.2 us (level)
  transfers between devices with their start and end apart: 17 -> 17, of which waited for: 7 -> 7; matrix products, arithmetic and copies ran while one was open for 0% -> 0% of each run, Pallas kernels for 11% -> 10%
where the time goes in v4:
time: 83.2 us; the launch traced here: 83 us
  starting transfers between devices  42.7 us (51%)
  waiting for transfers between devices  18.5 us (22%)
  Pallas kernels  15.9 us (19%)
  local copies, waits for them, and re-layouts  3.08 us (4%)
  other arithmetic  2.7 us (3%)
    ppermute x9, starting transfers between devices, from_chan(): lax.ppermute(block, 'chan', [(source(i), i) for i in range(chan_count)])  21.7 us
    pallas_call x2, Pallas kernels, edge(): pl.pallas_call(functools.partial(edge_body, not before), out_shape=(mine,...  14.4 us
    ppermute x3, waiting for transfers between devices, swap_freq(): return lax.ppermute(block, 'freq', [(0, 1), (1, 0)])  11.3 us
    ppermute x1, starting transfers between devices, sum_over_chan(): lax.ppermute(sums, ('chan', 'freq'), [(d, d ^ 2 * top ^ 1) for d in range...  7.96 us
    ppermute x2, starting transfers between devices, to_partner(): return lax.ppermute(block, ('chan', 'freq'), edge_route(size, flip))  7.44 us
    ppermute x9, waiting for transfers between devices, from_chan(): lax.ppermute(block, 'chan', [(source(i), i) for i in range(chan_count)])  6.65 us
    ppermute x3, starting transfers between devices, swap_freq(): return lax.ppermute(block, 'freq', [(0, 1), (1, 0)])  3.2 us
    unnamed x6, local copies, waits for them, and re-layouts  3.08 us
  transfers between devices with their start and end apart: 17, of which 7 were waited for; matrix products, arithmetic and copies ran while one was open for 0% of the time, Pallas kernels for 10%

profile of v4, /device:TPU:1, one launch (start us, length us, event | category | flops | bytes accessed | tf_op | source)
XLA Modules:
  0.0 83.0 jit_solution(8233076066061363582)
XLA Ops:
  0.0 1.3 %reduce_sum.9 = f32[2,16,256]{2,1,0:T(8,128)S(1)} reduce(f32[32,2,16,256]{3,2,1,0:T(8,128)} %raw.1, f32[]{:T(128)} %constant.47.clone.1), dimensions={0}, to_apply=%region_0.0 | reduce | flops 253952 | bytes 1081348 | tf_op jit(solution)/shard_map/reduce_sum | solution.py:334
  1.3 2.6 %collective-permute-start.1 = (f32[2,16,256]{2,1,0:T(8,128)S(1)}, f32[2,16,256]{2,1,0:T(8,128)S(1)}, u32[]{:S(2)}, u32[]{:S(2)}) collective-permute-start(f32[2,16,256]{2,1,0:T(8,128)S(1)} %reduce_sum.9), channel_id=1, source_target_pairs={{16,0},{18,2},{20,4},{22,6},{24,8},{26,10},{28,12},{30,14},{0,16},... | collective-permute-start | bytes 98312 | tf_op jit(solution)/shard_map/ppermute | solution.py:44
  3.9 2.7 %collective-permute-start = (f32[32,2,16,256]{3,2,1,0:T(8,128)}, f32[32,2,16,256]{3,2,1,0:T(8,128)S(1)}, u32[]{:S(2)}, u32[]{:S(2)}) collective-permute-start(f32[32,2,16,256]{3,2,1,0:T(8,128)} %raw.1), channel_id=1, source_target_pairs={{0,1},{1,0},{2,3},{3,2},{4,5},{5,4},{6,7},{7,6},{8,9},{9,8},{10,11... | collective-permute-start | bytes 3145736 | tf_op jit(solution)/shard_map/ppermute | solution.py:79
  6.6 0.0 collective-permute-done.1
  6.6 1.9 %collective-permute-start.2 = (f32[32,2,16,256]{3,2,1,0:T(8,128)}, f32[32,2,16,256]{3,2,1,0:T(8,128)S(1)}, u32[]{:S(2)}, u32[]{:S(2)}) collective-permute-start(f32[32,2,16,256]{3,2,1,0:T(8,128)} %raw.1), channel_id=1, source_target_pairs={{2,0},{5,1},{10,2},{19,3},{12,4},{21,5},{4,6},{3,7},{0,8},{25,9},{... | collective-permute-start | bytes 3145736 | tf_op jit(solution)/shard_map/ppermute | solution.py:328
  8.5 2.4 %collective-permute-start.5 = (f32[2,16,256]{2,1,0:T(8,128)S(1)}, f32[2,16,256]{2,1,0:T(8,128)S(1)}, u32[]{:S(2)}, u32[]{:S(2)}) collective-permute-start(f32[2,16,256]{2,1,0:T(8,128)S(1)} %add.46), channel_id=1, source_target_pairs={{96,0},{98,2},{100,4},{102,6},{104,8},{106,10},{108,12},{110,14},{... | collective-permute-start | bytes 98312 | tf_op jit(solution)/shard_map/ppermute | solution.py:44
  10.9 2.1 %collective-permute-start.4 = (f32[2,16,256]{2,1,0:T(8,128)S(1)}, f32[2,16,256]{2,1,0:T(8,128)S(1)}, u32[]{:S(2)}, u32[]{:S(2)}) collective-permute-start(f32[2,16,256]{2,1,0:T(8,128)S(1)} %add.46), channel_id=1, source_target_pairs={{32,0},{34,2},{36,4},{38,6},{40,8},{42,10},{44,12},{46,14},{48,16}... | collective-permute-start | bytes 98312 | tf_op jit(solution)/shard_map/ppermute | solution.py:44
  13.1 4.5 %collective-permute-start.3 = (f32[2,16,256]{2,1,0:T(8,128)S(1)}, f32[2,16,256]{2,1,0:T(8,128)S(1)}, u32[]{:S(2)}, u32[]{:S(2)}) collective-permute-start(f32[2,16,256]{2,1,0:T(8,128)S(1)} %add.46), channel_id=1, source_target_pairs={{64,0},{66,2},{68,4},{70,6},{72,8},{74,10},{76,12},{78,14},{80,16}... | collective-permute-start | bytes 98312 | tf_op jit(solution)/shard_map/ppermute | solution.py:44
  17.5 0.0 collective-permute-done.5
  17.5 0.0 collective-permute-done.4
  17.5 2.8 %collective-permute-done.3 = f32[2,16,256]{2,1,0:T(8,128)S(1)} collective-permute-done((f32[2,16,256]{2,1,0:T(8,128)S(1)}, f32[2,16,256]{2,1,0:T(8,128)S(1)}, u32[]{:S(2)}, u32[]{:S(2)}) %collective-permute-start.3) | collective-permute-done | bytes 32800 | tf_op jit(solution)/shard_map/ppermute | solution.py:44
  20.3 2.4 %collective-permute-start.8 = (f32[2,16,256]{2,1,0:T(8,128)S(1)}, f32[2,16,256]{2,1,0:T(8,128)S(1)}, u32[]{:S(2)}, u32[]{:S(2)}) collective-permute-start(f32[2,16,256]{2,1,0:T(8,128)S(1)} %add_add_fusion.1), channel_id=1, source_target_pairs={{12,0},{14,2},{0,4},{2,6},{4,8},{6,10},{8,12},{10,14},{28,16},{30,... | collective-permute-start | bytes 98312 | tf_op jit(solution)/shard_map/ppermute | solution.py:44
  22.7 0.3 collective-permute-start.7
  23.1 1.6 %collective-permute-start.6 = (f32[2,16,256]{2,1,0:T(8,128)S(1)}, f32[2,16,256]{2,1,0:T(8,128)S(1)}, u32[]{:S(2)}, u32[]{:S(2)}) collective-permute-start(f32[2,16,256]{2,1,0:T(8,128)S(1)} %add_add_fusion.1), channel_id=1, source_target_pairs={{8,0},{10,2},{12,4},{14,6},{0,8},{2,10},{4,12},{6,14},{24,16},{26,... | collective-permute-start | bytes 98312 | tf_op jit(solution)/shard_map/ppermute | solution.py:44
  24.6 0.0 collective-permute-done.8
  24.7 1.1 %collective-permute-done.7 = f32[2,16,256]{2,1,0:T(8,128)S(1)} collective-permute-done((f32[2,16,256]{2,1,0:T(8,128)S(1)}, f32[2,16,256]{2,1,0:T(8,128)S(1)}, u32[]{:S(2)}, u32[]{:S(2)}) %collective-permute-start.7) | collective-permute-done | bytes 32800 | tf_op jit(solution)/shard_map/ppermute | solution.py:44
  25.8 1.8 %collective-permute-done.6 = f32[2,16,256]{2,1,0:T(8,128)S(1)} collective-permute-done((f32[2,16,256]{2,1,0:T(8,128)S(1)}, f32[2,16,256]{2,1,0:T(8,128)S(1)}, u32[]{:S(2)}, u32[]{:S(2)}) %collective-permute-start.6) | collective-permute-done | bytes 32800 | tf_op jit(solution)/shard_map/ppermute | solution.py:44
  27.6 5.6 %collective-permute-start.9 = (f32[2,16,256]{2,1,0:T(8,128)S(1)}, f32[2,16,256]{2,1,0:T(8,128)S(1)}, u32[]{:S(2)}, u32[]{:S(2)}) collective-permute-start(f32[2,16,256]{2,1,0:T(8,128)S(1)} %add_add_fusion), channel_id=1, source_target_pairs={{2,0},{0,2},{6,4},{4,6},{10,8},{8,10},{14,12},{12,14},{18,16},{16,... | collective-permute-start | bytes 98312 | tf_op jit(solution)/shard_map/ppermute | solution.py:44
  33.2 0.9 %collective-permute-done.9 = f32[2,16,256]{2,1,0:T(8,128)S(1)} collective-permute-done((f32[2,16,256]{2,1,0:T(8,128)S(1)}, f32[2,16,256]{2,1,0:T(8,128)S(1)}, u32[]{:S(2)}, u32[]{:S(2)}) %collective-permute-start.9) | collective-permute-done | bytes 32800 | tf_op jit(solution)/shard_map/ppermute | solution.py:44
  34.1 0.0 collective-permute-done.other
  34.1 0.0 collective-permute-done.2.far0
  34.1 0.4 collective-permute-start.13
  34.5 0.1 add_add_fusion.2
  34.6 8.0 %collective-permute-start.12 = (f32[2,16,256]{2,1,0:T(8,128)S(1)}, f32[2,16,256]{2,1,0:T(8,128)S(1)}, u32[]{:S(2)}, u32[]{:S(2)}) collective-permute-start(f32[2,16,256]{2,1,0:T(8,128)S(1)} %add.53.sum0), channel_id=1, source_target_pairs={{0,129},{1,128},{2,131},{3,130},{4,133},{5,132},{6,135},{7,134},{8... | collective-permute-start | bytes 98312 | tf_op jit(solution)/shard_map/ppermute | solution.py:72
  42.5 0.4 collective-permute-start.11
  42.9 0.3 collective-permute-start.10
  43.2 0.1 add_add_fusion.3.place
  43.3 0.5 collective-permute-done.12.near1
  43.9 3.0 %collective-permute-done.11.sum1 = f32[2,16,256]{2,1,0:T(8,128)S(1)} collective-permute-done((f32[2,16,256]{2,1,0:T(8,128)S(1)}, f32[2,16,256]{2,1,0:T(8,128)S(1)}, u32[]{:S(2)}, u32[]{:S(2)}) %collective-permute-start.11) | collective-permute-done | bytes 32800 | tf_op jit(solution)/shard_map/ppermute | solution.py:79
  46.8 0.0 collective-permute-done.10.near0
  46.8 0.0 copy-start
  46.8 1.2 %copy-done = f32[32,2,16,256]{3,2,1,0:T(8,128)S(1)} copy-done((f32[32,2,16,256]{3,2,1,0:T(8,128)S(1)}, f32[32,2,16,256]{3,2,1,0:T(8,128)}, u32[]{:S(2)}) %copy-start) | copy-done | bytes 1048600
  48.0 0.0 copy-start.1
  48.0 1.1 %copy-done.1 = bf16[2,768,256]{2,1,0:T(8,128)(2,1)S(1)} copy-done((bf16[2,768,256]{2,1,0:T(8,128)(2,1)S(1)}, bf16[2,768,256]{2,1,0:T(8,128)(2,1)}, u32[]{:S(2)}) %copy-start.1) | copy-done | bytes 786456
  49.2 0.0 copy-start.2
  49.2 0.7 copy-done.2
  49.9 1.5 %own.1 = (f32[4,1536,128]{2,1,0:T(8,128)S(1)}, bf16[2,512,256]{2,1,0:T(8,128)(2,1)S(1)}, f32[32,128]{1,0:T(8,128)S(1)}, f32[32,128]{1,0:T(8,128)S(1)}) custom-call(s32[4]{0:T(128)S(1)} %add_add_fusion.3.place, f32[32,2,16,256]{3,2,1,0:T(8,128)S(1)} %copy-done, f32[32,2,16,256]{3,2,1,0:T(8,128)S(1)} %collective-permute-done.other, ...), custom_call_target="tpu_custom_call" | custom-call | tf_op jit(solution)/shard_map/own/pallas_call | solution.py:170
  51.5 0.0 collective-permute-done.13.far1
  51.5 7.3 %edge.2 = (f32[16,16,128]{2,1,0:T(8,128)S(1)}, f32[16,16,128]{2,1,0:T(8,128)S(1)}, f32[16,32,128]{2,1,0:T(8,128)S(1)}) custom-call(s32[4]{0:T(128)S(1)} %get-tuple-element.40.place, f32[4,1536,128]{2,1,0:T(8,128)S(1)} %get-tuple-element.26.a_rows, f32[32,2,16,256]{3,2,1,0:T(8,128)S(1)} %collective-permute-done.2.far0, ...), custom_call_target="tpu_custom_call" | custom-call | flops 1000000 | bytes 10000 | tf_op jit(solution)/shard_map/edge/pallas_call | solution.py:296
  58.7 6.2 %collective-permute-start.15 = (f32[16,32,128]{2,1,0:T(8,128)S(1)}, f32[16,32,128]{2,1,0:T(8,128)S(1)}, u32[]{:S(2)}, u32[]{:S(2)}) collective-permute-start(f32[16,32,128]{2,1,0:T(8,128)S(1)} %get-tuple-element.35), channel_id=1, source_target_pairs={{0,3},{1,4},{2,11},{3,18},{4,13},{5,20},{6,5},{7,2},{8,1},{9,24},{... | collective-permute-start | bytes 786440 | tf_op jit(solution)/shard_map/ppermute | solution.py:324
  64.9 7.1 %edge.3 = (f32[16,32,128]{2,1,0:T(8,128)S(1)}, f32[16,32,128]{2,1,0:T(8,128)S(1)}, f32[16,32,128]{2,1,0:T(8,128)S(1)}) custom-call(s32[4]{0:T(128)S(1)} %get-tuple-element.39.place, f32[4,1536,128]{2,1,0:T(8,128)S(1)} %get-tuple-element.26.a_rows, f32[32,2,16,256]{3,2,1,0:T(8,128)S(1)} %collective-permute-done.2.far0, ...), custom_call_target="tpu_custom_call" | custom-call | flops 1000000 | bytes 10000 | tf_op jit(solution)/shard_map/edge/pallas_call | solution.py:296
  72.1 0.1 collective-permute-start.14
  72.2 0.0 collective-permute-done.15
  72.2 1.2 %collective-permute-start.16 = (f32[16,32,128]{2,1,0:T(8,128)S(1)}, f32[16,32,128]{2,1,0:T(8,128)S(1)}, u32[]{:S(2)}, u32[]{:S(2)}) collective-permute-start(f32[16,32,128]{2,1,0:T(8,128)S(1)} %get-tuple-element.37), channel_id=1, source_target_pairs={{0,2},{1,5},{2,10},{3,19},{4,12},{5,21},{6,4},{7,3},{8,0},{9,25},{... | collective-permute-start | bytes 786440 | tf_op jit(solution)/shard_map/ppermute | solution.py:324
  73.4 8.3 %collective-permute-done.14 = f32[16,32,128]{2,1,0:T(8,128)S(1)} collective-permute-done((f32[16,32,128]{2,1,0:T(8,128)S(1)}, f32[16,32,128]{2,1,0:T(8,128)S(1)}, u32[]{:S(2)}, u32[]{:S(2)}) %collective-permute-start.14) | collective-permute-done | bytes 262176 | tf_op jit(solution)/shard_map/ppermute | solution.py:79
  81.8 0.0 collective-permute-done.16
  81.8 1.2 %select_select_fusion = f32[4,16,32,128]{3,2,1,0:T(8,128)} fusion(f32[16,32,128]{2,1,0:T(8,128)S(1)} %collective-permute-done.15, f32[16,32,128]{2,1,0:T(8,128)S(1)} %collective-permute-done.16, f32[16,32,128]{2,1,0:T(8,128)S(1)} %collective-permute-done.14, f32[16,32,128]{2,1,0:T(8,128)S(1)} %get-tuple-element.33, pred[4]{0:T(512)(128)(4,1)S(1)} %get-tuple-element.41, ...), kind=kLoop, calls=%fused_computation | loop fusion | flops 786432 | bytes 2097160 | tf_op jit(solution)/shard_map/jit(_where)/select_n | solution.py:373
  (5 shorter events, 0.0 us)
Async XLA Ops:
  1.3 5.3 %collective-permute-start.1 = (f32[2,16,256]{2,1,0:T(8,128)S(1)}, f32[2,16,256]{2,1,0:T(8,128)S(1)}, u32[]{:S(2)}, u32[]{:S(2)}) collective-permute-start(f32[2,16,256]{2,1,0:T(8,128)S(1)} %reduce_sum.9), channel_id=1, source_target_pairs={{16,0},{18,2},{20,4},{22,6},{24,8},{26,10},{28,12},{30,14},{0,16},... | collective-permute-start | bytes 98312 | tf_op jit(solution)/shard_map/ppermute | solution.py:44
  3.9 30.2 %collective-permute-start = (f32[32,2,16,256]{3,2,1,0:T(8,128)}, f32[32,2,16,256]{3,2,1,0:T(8,128)S(1)}, u32[]{:S(2)}, u32[]{:S(2)}) collective-permute-start(f32[32,2,16,256]{3,2,1,0:T(8,128)} %raw.1), channel_id=1, source_target_pairs={{0,1},{1,0},{2,3},{3,2},{4,5},{5,4},{6,7},{7,6},{8,9},{9,8},{10,11... | collective-permute-start | bytes 3145736 | tf_op jit(solution)/shard_map/ppermute | solution.py:79
  6.6 27.5 %collective-permute-start.2 = (f32[32,2,16,256]{3,2,1,0:T(8,128)}, f32[32,2,16,256]{3,2,1,0:T(8,128)S(1)}, u32[]{:S(2)}, u32[]{:S(2)}) collective-permute-start(f32[32,2,16,256]{3,2,1,0:T(8,128)} %raw.1), channel_id=1, source_target_pairs={{2,0},{5,1},{10,2},{19,3},{12,4},{21,5},{4,6},{3,7},{0,8},{25,9},{... | collective-permute-start | bytes 3145736 | tf_op jit(solution)/shard_map/ppermute | solution.py:328
  8.5 9.0 %collective-permute-start.5 = (f32[2,16,256]{2,1,0:T(8,128)S(1)}, f32[2,16,256]{2,1,0:T(8,128)S(1)}, u32[]{:S(2)}, u32[]{:S(2)}) collective-permute-start(f32[2,16,256]{2,1,0:T(8,128)S(1)} %add.46), channel_id=1, source_target_pairs={{96,0},{98,2},{100,4},{102,6},{104,8},{106,10},{108,12},{110,14},{... | collective-permute-start | bytes 98312 | tf_op jit(solution)/shard_map/ppermute | solution.py:44
  10.9 6.6 %collective-permute-start.4 = (f32[2,16,256]{2,1,0:T(8,128)S(1)}, f32[2,16,256]{2,1,0:T(8,128)S(1)}, u32[]{:S(2)}, u32[]{:S(2)}) collective-permute-start(f32[2,16,256]{2,1,0:T(8,128)S(1)} %add.46), channel_id=1, source_target_pairs={{32,0},{34,2},{36,4},{38,6},{40,8},{42,10},{44,12},{46,14},{48,16}... | collective-permute-start | bytes 98312 | tf_op jit(solution)/shard_map/ppermute | solution.py:44
  13.1 7.2 %collective-permute-start.3 = (f32[2,16,256]{2,1,0:T(8,128)S(1)}, f32[2,16,256]{2,1,0:T(8,128)S(1)}, u32[]{:S(2)}, u32[]{:S(2)}) collective-permute-start(f32[2,16,256]{2,1,0:T(8,128)S(1)} %add.46), channel_id=1, source_target_pairs={{64,0},{66,2},{68,4},{70,6},{72,8},{74,10},{76,12},{78,14},{80,16}... | collective-permute-start | bytes 98312 | tf_op jit(solution)/shard_map/ppermute | solution.py:44
  20.3 4.3 %collective-permute-start.8 = (f32[2,16,256]{2,1,0:T(8,128)S(1)}, f32[2,16,256]{2,1,0:T(8,128)S(1)}, u32[]{:S(2)}, u32[]{:S(2)}) collective-permute-start(f32[2,16,256]{2,1,0:T(8,128)S(1)} %add_add_fusion.1), channel_id=1, source_target_pairs={{12,0},{14,2},{0,4},{2,6},{4,8},{6,10},{8,12},{10,14},{28,16},{30,... | collective-permute-start | bytes 98312 | tf_op jit(solution)/shard_map/ppermute | solution.py:44
  22.7 3.1 %collective-permute-start.7 = (f32[2,16,256]{2,1,0:T(8,128)S(1)}, f32[2,16,256]{2,1,0:T(8,128)S(1)}, u32[]{:S(2)}, u32[]{:S(2)}) collective-permute-start(f32[2,16,256]{2,1,0:T(8,128)S(1)} %add_add_fusion.1), channel_id=1, source_target_pairs={{4,0},{6,2},{8,4},{10,6},{12,8},{14,10},{0,12},{2,14},{20,16},{22,... | collective-permute-start | bytes 98312 | tf_op jit(solution)/shard_map/ppermute | solution.py:44
  23.1 4.6 %collective-permute-start.6 = (f32[2,16,256]{2,1,0:T(8,128)S(1)}, f32[2,16,256]{2,1,0:T(8,128)S(1)}, u32[]{:S(2)}, u32[]{:S(2)}) collective-permute-start(f32[2,16,256]{2,1,0:T(8,128)S(1)} %add_add_fusion.1), channel_id=1, source_target_pairs={{8,0},{10,2},{12,4},{14,6},{0,8},{2,10},{4,12},{6,14},{24,16},{26,... | collective-permute-start | bytes 98312 | tf_op jit(solution)/shard_map/ppermute | solution.py:44
  27.6 6.4 %collective-permute-start.9 = (f32[2,16,256]{2,1,0:T(8,128)S(1)}, f32[2,16,256]{2,1,0:T(8,128)S(1)}, u32[]{:S(2)}, u32[]{:S(2)}) collective-permute-start(f32[2,16,256]{2,1,0:T(8,128)S(1)} %add_add_fusion), channel_id=1, source_target_pairs={{2,0},{0,2},{6,4},{4,6},{10,8},{8,10},{14,12},{12,14},{18,16},{16,... | collective-permute-start | bytes 98312 | tf_op jit(solution)/shard_map/ppermute | solution.py:44
  34.1 17.4 %collective-permute-start.13 = (f32[32,2,16,256]{3,2,1,0:T(8,128)S(1)}, f32[32,2,16,256]{3,2,1,0:T(8,128)S(1)}, u32[]{:S(2)}, u32[]{:S(2)}) collective-permute-start(f32[32,2,16,256]{3,2,1,0:T(8,128)S(1)} %collective-permute-done.other), channel_id=1, source_target_pairs={{2,0},{5,1},{10,2},{19,3},{12,4},{21,5},{4,6},{3,7},{0,8},{25,9},{... | collective-permute-start | bytes 3145736 | tf_op jit(solution)/shard_map/ppermute | solution.py:328
  34.6 9.3 %collective-permute-start.12 = (f32[2,16,256]{2,1,0:T(8,128)S(1)}, f32[2,16,256]{2,1,0:T(8,128)S(1)}, u32[]{:S(2)}, u32[]{:S(2)}) collective-permute-start(f32[2,16,256]{2,1,0:T(8,128)S(1)} %add.53.sum0), channel_id=1, source_target_pairs={{0,129},{1,128},{2,131},{3,130},{4,133},{5,132},{6,135},{7,134},{8... | collective-permute-start | bytes 98312 | tf_op jit(solution)/shard_map/ppermute | solution.py:72
  42.5 4.3 %collective-permute-start.11 = (f32[2,16,256]{2,1,0:T(8,128)S(1)}, f32[2,16,256]{2,1,0:T(8,128)S(1)}, u32[]{:S(2)}, u32[]{:S(2)}) collective-permute-start(f32[2,16,256]{2,1,0:T(8,128)S(1)} %add.53.sum0), channel_id=1, source_target_pairs={{0,1},{1,0},{2,3},{3,2},{4,5},{5,4},{6,7},{7,6},{8,9},{9,8},{10,11... | collective-permute-start | bytes 98312 | tf_op jit(solution)/shard_map/ppermute | solution.py:79
  42.9 3.9 %collective-permute-start.10 = (f32[2,16,256]{2,1,0:T(8,128)S(1)}, f32[2,16,256]{2,1,0:T(8,128)S(1)}, u32[]{:S(2)}, u32[]{:S(2)}) collective-permute-start(f32[2,16,256]{2,1,0:T(8,128)S(1)} %add.53.sum0), channel_id=1, source_target_pairs={{128,0},{130,2},{132,4},{134,6},{136,8},{138,10},{140,12},{142,14}... | collective-permute-start | bytes 98312 | tf_op jit(solution)/shard_map/ppermute | solution.py:44
  46.8 1.2 %copy-start = (f32[32,2,16,256]{3,2,1,0:T(8,128)S(1)}, f32[32,2,16,256]{3,2,1,0:T(8,128)}, u32[]{:S(2)}) copy-start(f32[32,2,16,256]{3,2,1,0:T(8,128)} %raw.1) | copy-start | bytes 3145732
  48.0 1.1 %copy-start.1 = (bf16[2,768,256]{2,1,0:T(8,128)(2,1)S(1)}, bf16[2,768,256]{2,1,0:T(8,128)(2,1)}, u32[]{:S(2)}) copy-start(bf16[2,768,256]{2,1,0:T(8,128)(2,1)} %constant.48.clone.all_tables) | copy-start | bytes 2359300
  49.2 0.7 copy-start.2
  58.7 13.4 %collective-permute-start.15 = (f32[16,32,128]{2,1,0:T(8,128)S(1)}, f32[16,32,128]{2,1,0:T(8,128)S(1)}, u32[]{:S(2)}, u32[]{:S(2)}) collective-permute-start(f32[16,32,128]{2,1,0:T(8,128)S(1)} %get-tuple-element.35), channel_id=1, source_target_pairs={{0,3},{1,4},{2,11},{3,18},{4,13},{5,20},{6,5},{7,2},{8,1},{9,24},{... | collective-permute-start | bytes 786440 | tf_op jit(solution)/shard_map/ppermute | solution.py:324
  72.1 9.7 %collective-permute-start.14 = (f32[16,32,128]{2,1,0:T(8,128)S(1)}, f32[16,32,128]{2,1,0:T(8,128)S(1)}, u32[]{:S(2)}, u32[]{:S(2)}) collective-permute-start(f32[16,32,128]{2,1,0:T(8,128)S(1)} %get-tuple-element.34), channel_id=1, source_target_pairs={{0,1},{1,0},{2,3},{3,2},{4,5},{5,4},{6,7},{7,6},{8,9},{9,8},{10,11... | collective-permute-start | bytes 786440 | tf_op jit(solution)/shard_map/ppermute | solution.py:79
  72.2 9.6 %collective-permute-start.16 = (f32[16,32,128]{2,1,0:T(8,128)S(1)}, f32[16,32,128]{2,1,0:T(8,128)S(1)}, u32[]{:S(2)}, u32[]{:S(2)}) collective-permute-start(f32[16,32,128]{2,1,0:T(8,128)S(1)} %get-tuple-element.37), channel_id=1, source_target_pairs={{0,2},{1,5},{2,10},{3,19},{4,12},{5,21},{6,4},{7,3},{8,0},{9,25},{... | collective-permute-start | bytes 786440 | tf_op jit(solution)/shard_map/ppermute | solution.py:324

commit v5 on v4

--- a/solution.py
+++ b/solution.py
@@ -129,6 +129,7 @@
     a_rows, table, own_n, far_n, buf, sem, table_sem,
 ):
     chans, _, _, half = raw.shape
+    hrows = chans // 2
     step = 8
     fetches = []
     for c in range(chans // step):
@@ -137,11 +138,17 @@
             fetches.append(pltpu.make_async_copy(source.at[at], buf.at[k, at], sem.at[k, c]))
     for fetch in fetches:
         fetch.start()
-    first_bin = pl.multiple_of(place[1] * (half // (chans // 2)), half)
-    table_fetch = pltpu.make_async_copy(
-        all_tables.at[:, pl.ds(first_bin, 2 * half), :], table, table_sem
-    )
-    table_fetch.start()
+    first_bin = pl.multiple_of(place[1] * (half // hrows), half)
+    table_fetches = [
+        pltpu.make_async_copy(
+            all_tables.at[:, pl.ds(bin_at, half), :],
+            table.at[:, k * half : (k + 1) * half, :],
+            table_sem.at[k],
+        )
+        for k, bin_at in enumerate((first_bin, pl.multiple_of(half - first_bin, half)))
+    ]
+    for fetch in table_fetches:
+        fetch.start()
     own_n[...] = jnp.broadcast_to(channel_counts(windows, place[2], chans), (chans, LANE))
     far_n[...] = jnp.broadcast_to(channel_counts(windows, place[3], chans), (chans, LANE))
     mean = means((sum0, near0, sum1, near1))
@@ -159,7 +166,8 @@
             return carry
 
         lax.fori_loop(0, step, channel, 0, unroll=True)
-    table_fetch.wait()
+    for fetch in table_fetches:
+        fetch.wait()
 
 
 def whiten_own(place, raw, other, sums, windows, all_tables):
@@ -180,7 +188,7 @@
         scratch_shapes=[
             pltpu.VMEM((2, *raw.shape), F32),
             pltpu.SemaphoreType.DMA((2, chans // 8)),
-            pltpu.SemaphoreType.DMA,
+            pltpu.SemaphoreType.DMA((2,)),
         ],
         compiler_params=pltpu.CompilerParams(vmem_limit_bytes=12 * 1024 * 1024),
         name="own",
@@ -353,8 +361,7 @@
     def at(b0):
         return jnp.stack([b0, freq_index * hrows, chan_index, partner]).astype(jnp.int32)
 
-    all_tables = np.stack(lag_tables())
-    all_tables = jnp.asarray(np.concatenate([all_tables, all_tables[:, :half]], axis=1))
+    all_tables = jnp.asarray(np.stack(lag_tables()))
     a_rows, table, *counts = whiten_own(at(0), raw_spectra, far["own"], sums, windows, all_tables)
 
     def work(b0, before=()):

time: 83.2 us -> 83.2 us (level)
  no operation moved by 1% of the time
where the time goes in v5:
time: 83.2 us; the launch traced here: 83 us
  starting transfers between devices  42.8 us (51%)
  waiting for transfers between devices  18.5 us (22%)
  Pallas kernels  15.9 us (19%)
  local copies, waits for them, and re-layouts  2.98 us (4%)
  other arithmetic  2.7 us (3%)
    ppermute x9, starting transfers between devices, from_chan(): lax.ppermute(block, 'chan', [(source(i), i) for i in range(chan_count)])  21.7 us
    pallas_call x2, Pallas kernels, edge(): pl.pallas_call(functools.partial(edge_body, not before), out_shape=(mine,...  14.4 us
    ppermute x3, waiting for transfers between devices, swap_freq(): return lax.ppermute(block, 'freq', [(0, 1), (1, 0)])  11.3 us
    ppermute x1, starting transfers between devices, sum_over_chan(): lax.ppermute(sums, ('chan', 'freq'), [(d, d ^ 2 * top ^ 1) for d in range...  7.96 us
    ppermute x2, starting transfers between devices, to_partner(): return lax.ppermute(block, ('chan', 'freq'), edge_route(size, flip))  7.52 us
    ppermute x9, waiting for transfers between devices, from_chan(): lax.ppermute(block, 'chan', [(source(i), i) for i in range(chan_count)])  6.65 us
    ppermute x3, starting transfers between devices, swap_freq(): return lax.ppermute(block, 'freq', [(0, 1), (1, 0)])  3.2 us
    unnamed x6, local copies, waits for them, and re-layouts  2.98 us
  transfers between devices with their start and end apart: 17, of which 7 were waited for; matrix products, arithmetic and copies ran while one was open for 0% of the time, Pallas kernels for 10%

profile of v5, /device:TPU:1, one launch (start us, length us, event | category | flops | bytes accessed | tf_op | source)
XLA Modules:
  0.0 83.0 jit_solution(12575420813875992053)
XLA Ops:
  0.0 1.3 %reduce_sum.9 = f32[2,16,256]{2,1,0:T(8,128)S(1)} reduce(f32[32,2,16,256]{3,2,1,0:T(8,128)} %raw.1, f32[]{:T(128)} %constant.47.clone.1), dimensions={0}, to_apply=%region_0.0 | reduce | flops 253952 | bytes 1081348 | tf_op jit(solution)/shard_map/reduce_sum | solution.py:342
  1.3 2.6 %collective-permute-start.1 = (f32[2,16,256]{2,1,0:T(8,128)S(1)}, f32[2,16,256]{2,1,0:T(8,128)S(1)}, u32[]{:S(2)}, u32[]{:S(2)}) collective-permute-start(f32[2,16,256]{2,1,0:T(8,128)S(1)} %reduce_sum.9), channel_id=1, source_target_pairs={{16,0},{18,2},{20,4},{22,6},{24,8},{26,10},{28,12},{30,14},{0,16},... | collective-permute-start | bytes 98312 | tf_op jit(solution)/shard_map/ppermute | solution.py:44
  3.9 2.7 %collective-permute-start = (f32[32,2,16,256]{3,2,1,0:T(8,128)}, f32[32,2,16,256]{3,2,1,0:T(8,128)S(1)}, u32[]{:S(2)}, u32[]{:S(2)}) collective-permute-start(f32[32,2,16,256]{3,2,1,0:T(8,128)} %raw.1), channel_id=1, source_target_pairs={{0,1},{1,0},{2,3},{3,2},{4,5},{5,4},{6,7},{7,6},{8,9},{9,8},{10,11... | collective-permute-start | bytes 3145736 | tf_op jit(solution)/shard_map/ppermute | solution.py:79
  6.6 0.0 collective-permute-done.1
  6.6 1.9 %collective-permute-start.2 = (f32[32,2,16,256]{3,2,1,0:T(8,128)}, f32[32,2,16,256]{3,2,1,0:T(8,128)S(1)}, u32[]{:S(2)}, u32[]{:S(2)}) collective-permute-start(f32[32,2,16,256]{3,2,1,0:T(8,128)} %raw.1), channel_id=1, source_target_pairs={{2,0},{5,1},{10,2},{19,3},{12,4},{21,5},{4,6},{3,7},{0,8},{25,9},{... | collective-permute-start | bytes 3145736 | tf_op jit(solution)/shard_map/ppermute | solution.py:336
  8.5 2.4 %collective-permute-start.5 = (f32[2,16,256]{2,1,0:T(8,128)S(1)}, f32[2,16,256]{2,1,0:T(8,128)S(1)}, u32[]{:S(2)}, u32[]{:S(2)}) collective-permute-start(f32[2,16,256]{2,1,0:T(8,128)S(1)} %add.46), channel_id=1, source_target_pairs={{96,0},{98,2},{100,4},{102,6},{104,8},{106,10},{108,12},{110,14},{... | collective-permute-start | bytes 98312 | tf_op jit(solution)/shard_map/ppermute | solution.py:44
  10.9 2.1 %collective-permute-start.4 = (f32[2,16,256]{2,1,0:T(8,128)S(1)}, f32[2,16,256]{2,1,0:T(8,128)S(1)}, u32[]{:S(2)}, u32[]{:S(2)}) collective-permute-start(f32[2,16,256]{2,1,0:T(8,128)S(1)} %add.46), channel_id=1, source_target_pairs={{32,0},{34,2},{36,4},{38,6},{40,8},{42,10},{44,12},{46,14},{48,16}... | collective-permute-start | bytes 98312 | tf_op jit(solution)/shard_map/ppermute | solution.py:44
  13.1 4.5 %collective-permute-start.3 = (f32[2,16,256]{2,1,0:T(8,128)S(1)}, f32[2,16,256]{2,1,0:T(8,128)S(1)}, u32[]{:S(2)}, u32[]{:S(2)}) collective-permute-start(f32[2,16,256]{2,1,0:T(8,128)S(1)} %add.46), channel_id=1, source_target_pairs={{64,0},{66,2},{68,4},{70,6},{72,8},{74,10},{76,12},{78,14},{80,16}... | collective-permute-start | bytes 98312 | tf_op jit(solution)/shard_map/ppermute | solution.py:44
  17.5 0.0 collective-permute-done.5
  17.5 0.0 collective-permute-done.4
  17.5 2.8 %collective-permute-done.3 = f32[2,16,256]{2,1,0:T(8,128)S(1)} collective-permute-done((f32[2,16,256]{2,1,0:T(8,128)S(1)}, f32[2,16,256]{2,1,0:T(8,128)S(1)}, u32[]{:S(2)}, u32[]{:S(2)}) %collective-permute-start.3) | collective-permute-done | bytes 32800 | tf_op jit(solution)/shard_map/ppermute | solution.py:44
  20.3 2.4 %collective-permute-start.8 = (f32[2,16,256]{2,1,0:T(8,128)S(1)}, f32[2,16,256]{2,1,0:T(8,128)S(1)}, u32[]{:S(2)}, u32[]{:S(2)}) collective-permute-start(f32[2,16,256]{2,1,0:T(8,128)S(1)} %add_add_fusion.1), channel_id=1, source_target_pairs={{12,0},{14,2},{0,4},{2,6},{4,8},{6,10},{8,12},{10,14},{28,16},{30,... | collective-permute-start | bytes 98312 | tf_op jit(solution)/shard_map/ppermute | solution.py:44
  22.7 0.3 collective-permute-start.7
  23.1 1.6 %collective-permute-start.6 = (f32[2,16,256]{2,1,0:T(8,128)S(1)}, f32[2,16,256]{2,1,0:T(8,128)S(1)}, u32[]{:S(2)}, u32[]{:S(2)}) collective-permute-start(f32[2,16,256]{2,1,0:T(8,128)S(1)} %add_add_fusion.1), channel_id=1, source_target_pairs={{8,0},{10,2},{12,4},{14,6},{0,8},{2,10},{4,12},{6,14},{24,16},{26,... | collective-permute-start | bytes 98312 | tf_op jit(solution)/shard_map/ppermute | solution.py:44
  24.6 0.0 collective-permute-done.8
  24.7 1.1 %collective-permute-done.7 = f32[2,16,256]{2,1,0:T(8,128)S(1)} collective-permute-done((f32[2,16,256]{2,1,0:T(8,128)S(1)}, f32[2,16,256]{2,1,0:T(8,128)S(1)}, u32[]{:S(2)}, u32[]{:S(2)}) %collective-permute-start.7) | collective-permute-done | bytes 32800 | tf_op jit(solution)/shard_map/ppermute | solution.py:44
  25.8 1.8 %collective-permute-done.6 = f32[2,16,256]{2,1,0:T(8,128)S(1)} collective-permute-done((f32[2,16,256]{2,1,0:T(8,128)S(1)}, f32[2,16,256]{2,1,0:T(8,128)S(1)}, u32[]{:S(2)}, u32[]{:S(2)}) %collective-permute-start.6) | collective-permute-done | bytes 32800 | tf_op jit(solution)/shard_map/ppermute | solution.py:44
  27.6 5.6 %collective-permute-start.9 = (f32[2,16,256]{2,1,0:T(8,128)S(1)}, f32[2,16,256]{2,1,0:T(8,128)S(1)}, u32[]{:S(2)}, u32[]{:S(2)}) collective-permute-start(f32[2,16,256]{2,1,0:T(8,128)S(1)} %add_add_fusion), channel_id=1, source_target_pairs={{2,0},{0,2},{6,4},{4,6},{10,8},{8,10},{14,12},{12,14},{18,16},{16,... | collective-permute-start | bytes 98312 | tf_op jit(solution)/shard_map/ppermute | solution.py:44
  33.2 0.9 %collective-permute-done.9 = f32[2,16,256]{2,1,0:T(8,128)S(1)} collective-permute-done((f32[2,16,256]{2,1,0:T(8,128)S(1)}, f32[2,16,256]{2,1,0:T(8,128)S(1)}, u32[]{:S(2)}, u32[]{:S(2)}) %collective-permute-start.9) | collective-permute-done | bytes 32800 | tf_op jit(solution)/shard_map/ppermute | solution.py:44
  34.1 0.0 collective-permute-done.other
  34.1 0.0 collective-permute-done.2.far0
  34.1 0.4 collective-permute-start.13
  34.5 0.1 add_add_fusion.2
  34.6 8.0 %collective-permute-start.12 = (f32[2,16,256]{2,1,0:T(8,128)S(1)}, f32[2,16,256]{2,1,0:T(8,128)S(1)}, u32[]{:S(2)}, u32[]{:S(2)}) collective-permute-start(f32[2,16,256]{2,1,0:T(8,128)S(1)} %add.53.sum0), channel_id=1, source_target_pairs={{0,129},{1,128},{2,131},{3,130},{4,133},{5,132},{6,135},{7,134},{8... | collective-permute-start | bytes 98312 | tf_op jit(solution)/shard_map/ppermute | solution.py:72
  42.5 0.4 collective-permute-start.11
  42.9 0.3 collective-permute-start.10
  43.2 0.1 add_add_fusion.3.place
  43.3 0.5 collective-permute-done.12.near1
  43.9 3.0 %collective-permute-done.11.sum1 = f32[2,16,256]{2,1,0:T(8,128)S(1)} collective-permute-done((f32[2,16,256]{2,1,0:T(8,128)S(1)}, f32[2,16,256]{2,1,0:T(8,128)S(1)}, u32[]{:S(2)}, u32[]{:S(2)}) %collective-permute-start.11) | collective-permute-done | bytes 32800 | tf_op jit(solution)/shard_map/ppermute | solution.py:79
  46.8 0.0 collective-permute-done.10.near0
  46.8 0.0 copy-start
  46.8 1.2 %copy-done = f32[32,2,16,256]{3,2,1,0:T(8,128)S(1)} copy-done((f32[32,2,16,256]{3,2,1,0:T(8,128)S(1)}, f32[32,2,16,256]{3,2,1,0:T(8,128)}, u32[]{:S(2)}) %copy-start) | copy-done | bytes 1048600
  48.0 0.0 copy-start.1
  48.0 1.0 %copy-done.1 = bf16[2,512,256]{2,1,0:T(8,128)(2,1)S(1)} copy-done((bf16[2,512,256]{2,1,0:T(8,128)(2,1)S(1)}, bf16[2,512,256]{2,1,0:T(8,128)(2,1)}, u32[]{:S(2)}) %copy-start.1) | copy-done | bytes 524312
  49.1 0.0 copy-start.2
  49.1 0.7 copy-done.2
  49.8 1.6 %own.1 = (f32[4,1536,128]{2,1,0:T(8,128)S(1)}, bf16[2,512,256]{2,1,0:T(8,128)(2,1)S(1)}, f32[32,128]{1,0:T(8,128)S(1)}, f32[32,128]{1,0:T(8,128)S(1)}) custom-call(s32[4]{0:T(128)S(1)} %add_add_fusion.3.place, f32[32,2,16,256]{3,2,1,0:T(8,128)S(1)} %copy-done, f32[32,2,16,256]{3,2,1,0:T(8,128)S(1)} %collective-permute-done.other, ...), custom_call_target="tpu_custom_call" | custom-call | tf_op jit(solution)/shard_map/own/pallas_call | solution.py:178
  51.4 0.0 collective-permute-done.13.far1
  51.4 7.3 %edge.2 = (f32[16,16,128]{2,1,0:T(8,128)S(1)}, f32[16,16,128]{2,1,0:T(8,128)S(1)}, f32[16,32,128]{2,1,0:T(8,128)S(1)}) custom-call(s32[4]{0:T(128)S(1)} %get-tuple-element.40.place, f32[4,1536,128]{2,1,0:T(8,128)S(1)} %get-tuple-element.26.a_rows, f32[32,2,16,256]{3,2,1,0:T(8,128)S(1)} %collective-permute-done.2.far0, ...), custom_call_target="tpu_custom_call" | custom-call | flops 1000000 | bytes 10000 | tf_op jit(solution)/shard_map/edge/pallas_call | solution.py:304
  58.7 6.3 %collective-permute-start.15 = (f32[16,32,128]{2,1,0:T(8,128)S(1)}, f32[16,32,128]{2,1,0:T(8,128)S(1)}, u32[]{:S(2)}, u32[]{:S(2)}) collective-permute-start(f32[16,32,128]{2,1,0:T(8,128)S(1)} %get-tuple-element.35), channel_id=1, source_target_pairs={{0,3},{1,4},{2,11},{3,18},{4,13},{5,20},{6,5},{7,2},{8,1},{9,24},{... | collective-permute-start | bytes 786440 | tf_op jit(solution)/shard_map/ppermute | solution.py:332
  64.9 7.1 %edge.3 = (f32[16,32,128]{2,1,0:T(8,128)S(1)}, f32[16,32,128]{2,1,0:T(8,128)S(1)}, f32[16,32,128]{2,1,0:T(8,128)S(1)}) custom-call(s32[4]{0:T(128)S(1)} %get-tuple-element.39.place, f32[4,1536,128]{2,1,0:T(8,128)S(1)} %get-tuple-element.26.a_rows, f32[32,2,16,256]{3,2,1,0:T(8,128)S(1)} %collective-permute-done.2.far0, ...), custom_call_target="tpu_custom_call" | custom-call | flops 1000000 | bytes 10000 | tf_op jit(solution)/shard_map/edge/pallas_call | solution.py:304
  72.1 0.1 collective-permute-start.14
  72.2 0.0 collective-permute-done.15
  72.2 1.2 %collective-permute-start.16 = (f32[16,32,128]{2,1,0:T(8,128)S(1)}, f32[16,32,128]{2,1,0:T(8,128)S(1)}, u32[]{:S(2)}, u32[]{:S(2)}) collective-permute-start(f32[16,32,128]{2,1,0:T(8,128)S(1)} %get-tuple-element.37), channel_id=1, source_target_pairs={{0,2},{1,5},{2,10},{3,19},{4,12},{5,21},{6,4},{7,3},{8,0},{9,25},{... | collective-permute-start | bytes 786440 | tf_op jit(solution)/shard_map/ppermute | solution.py:332
  73.4 8.3 %collective-permute-done.14 = f32[16,32,128]{2,1,0:T(8,128)S(1)} collective-permute-done((f32[16,32,128]{2,1,0:T(8,128)S(1)}, f32[16,32,128]{2,1,0:T(8,128)S(1)}, u32[]{:S(2)}, u32[]{:S(2)}) %collective-permute-start.14) | collective-permute-done | bytes 262176 | tf_op jit(solution)/shard_map/ppermute | solution.py:79
  81.8 0.0 collective-permute-done.16
  81.8 1.2 %select_select_fusion = f32[4,16,32,128]{3,2,1,0:T(8,128)} fusion(f32[16,32,128]{2,1,0:T(8,128)S(1)} %collective-permute-done.15, f32[16,32,128]{2,1,0:T(8,128)S(1)} %collective-permute-done.16, f32[16,32,128]{2,1,0:T(8,128)S(1)} %collective-permute-done.14, f32[16,32,128]{2,1,0:T(8,128)S(1)} %get-tuple-element.33, pred[4]{0:T(512)(128)(4,1)S(1)} %get-tuple-element.41, ...), kind=kLoop, calls=%fused_computation | loop fusion | flops 786432 | bytes 2097160 | tf_op jit(solution)/shard_map/jit(_where)/select_n | solution.py:380
  (5 shorter events, 0.0 us)
Async XLA Ops:
  1.3 5.3 %collective-permute-start.1 = (f32[2,16,256]{2,1,0:T(8,128)S(1)}, f32[2,16,256]{2,1,0:T(8,128)S(1)}, u32[]{:S(2)}, u32[]{:S(2)}) collective-permute-start(f32[2,16,256]{2,1,0:T(8,128)S(1)} %reduce_sum.9), channel_id=1, source_target_pairs={{16,0},{18,2},{20,4},{22,6},{24,8},{26,10},{28,12},{30,14},{0,16},... | collective-permute-start | bytes 98312 | tf_op jit(solution)/shard_map/ppermute | solution.py:44
  3.9 30.2 %collective-permute-start = (f32[32,2,16,256]{3,2,1,0:T(8,128)}, f32[32,2,16,256]{3,2,1,0:T(8,128)S(1)}, u32[]{:S(2)}, u32[]{:S(2)}) collective-permute-start(f32[32,2,16,256]{3,2,1,0:T(8,128)} %raw.1), channel_id=1, source_target_pairs={{0,1},{1,0},{2,3},{3,2},{4,5},{5,4},{6,7},{7,6},{8,9},{9,8},{10,11... | collective-permute-start | bytes 3145736 | tf_op jit(solution)/shard_map/ppermute | solution.py:79
  6.6 27.5 %collective-permute-start.2 = (f32[32,2,16,256]{3,2,1,0:T(8,128)}, f32[32,2,16,256]{3,2,1,0:T(8,128)S(1)}, u32[]{:S(2)}, u32[]{:S(2)}) collective-permute-start(f32[32,2,16,256]{3,2,1,0:T(8,128)} %raw.1), channel_id=1, source_target_pairs={{2,0},{5,1},{10,2},{19,3},{12,4},{21,5},{4,6},{3,7},{0,8},{25,9},{... | collective-permute-start | bytes 3145736 | tf_op jit(solution)/shard_map/ppermute | solution.py:336
  8.5 9.0 %collective-permute-start.5 = (f32[2,16,256]{2,1,0:T(8,128)S(1)}, f32[2,16,256]{2,1,0:T(8,128)S(1)}, u32[]{:S(2)}, u32[]{:S(2)}) collective-permute-start(f32[2,16,256]{2,1,0:T(8,128)S(1)} %add.46), channel_id=1, source_target_pairs={{96,0},{98,2},{100,4},{102,6},{104,8},{106,10},{108,12},{110,14},{... | collective-permute-start | bytes 98312 | tf_op jit(solution)/shard_map/ppermute | solution.py:44
  10.9 6.6 %collective-permute-start.4 = (f32[2,16,256]{2,1,0:T(8,128)S(1)}, f32[2,16,256]{2,1,0:T(8,128)S(1)}, u32[]{:S(2)}, u32[]{:S(2)}) collective-permute-start(f32[2,16,256]{2,1,0:T(8,128)S(1)} %add.46), channel_id=1, source_target_pairs={{32,0},{34,2},{36,4},{38,6},{40,8},{42,10},{44,12},{46,14},{48,16}... | collective-permute-start | bytes 98312 | tf_op jit(solution)/shard_map/ppermute | solution.py:44
  13.1 7.2 %collective-permute-start.3 = (f32[2,16,256]{2,1,0:T(8,128)S(1)}, f32[2,16,256]{2,1,0:T(8,128)S(1)}, u32[]{:S(2)}, u32[]{:S(2)}) collective-permute-start(f32[2,16,256]{2,1,0:T(8,128)S(1)} %add.46), channel_id=1, source_target_pairs={{64,0},{66,2},{68,4},{70,6},{72,8},{74,10},{76,12},{78,14},{80,16}... | collective-permute-start | bytes 98312 | tf_op jit(solution)/shard_map/ppermute | solution.py:44
  20.3 4.3 %collective-permute-start.8 = (f32[2,16,256]{2,1,0:T(8,128)S(1)}, f32[2,16,256]{2,1,0:T(8,128)S(1)}, u32[]{:S(2)}, u32[]{:S(2)}) collective-permute-start(f32[2,16,256]{2,1,0:T(8,128)S(1)} %add_add_fusion.1), channel_id=1, source_target_pairs={{12,0},{14,2},{0,4},{2,6},{4,8},{6,10},{8,12},{10,14},{28,16},{30,... | collective-permute-start | bytes 98312 | tf_op jit(solution)/shard_map/ppermute | solution.py:44
  22.7 3.1 %collective-permute-start.7 = (f32[2,16,256]{2,1,0:T(8,128)S(1)}, f32[2,16,256]{2,1,0:T(8,128)S(1)}, u32[]{:S(2)}, u32[]{:S(2)}) collective-permute-start(f32[2,16,256]{2,1,0:T(8,128)S(1)} %add_add_fusion.1), channel_id=1, source_target_pairs={{4,0},{6,2},{8,4},{10,6},{12,8},{14,10},{0,12},{2,14},{20,16},{22,... | collective-permute-start | bytes 98312 | tf_op jit(solution)/shard_map/ppermute | solution.py:44
  23.1 4.6 %collective-permute-start.6 = (f32[2,16,256]{2,1,0:T(8,128)S(1)}, f32[2,16,256]{2,1,0:T(8,128)S(1)}, u32[]{:S(2)}, u32[]{:S(2)}) collective-permute-start(f32[2,16,256]{2,1,0:T(8,128)S(1)} %add_add_fusion.1), channel_id=1, source_target_pairs={{8,0},{10,2},{12,4},{14,6},{0,8},{2,10},{4,12},{6,14},{24,16},{26,... | collective-permute-start | bytes 98312 | tf_op jit(solution)/shard_map/ppermute | solution.py:44
  27.6 6.4 %collective-permute-start.9 = (f32[2,16,256]{2,1,0:T(8,128)S(1)}, f32[2,16,256]{2,1,0:T(8,128)S(1)}, u32[]{:S(2)}, u32[]{:S(2)}) collective-permute-start(f32[2,16,256]{2,1,0:T(8,128)S(1)} %add_add_fusion), channel_id=1, source_target_pairs={{2,0},{0,2},{6,4},{4,6},{10,8},{8,10},{14,12},{12,14},{18,16},{16,... | collective-permute-start | bytes 98312 | tf_op jit(solution)/shard_map/ppermute | solution.py:44
  34.1 17.3 %collective-permute-start.13 = (f32[32,2,16,256]{3,2,1,0:T(8,128)S(1)}, f32[32,2,16,256]{3,2,1,0:T(8,128)S(1)}, u32[]{:S(2)}, u32[]{:S(2)}) collective-permute-start(f32[32,2,16,256]{3,2,1,0:T(8,128)S(1)} %collective-permute-done.other), channel_id=1, source_target_pairs={{2,0},{5,1},{10,2},{19,3},{12,4},{21,5},{4,6},{3,7},{0,8},{25,9},{... | collective-permute-start | bytes 3145736 | tf_op jit(solution)/shard_map/ppermute | solution.py:336
  34.6 9.3 %collective-permute-start.12 = (f32[2,16,256]{2,1,0:T(8,128)S(1)}, f32[2,16,256]{2,1,0:T(8,128)S(1)}, u32[]{:S(2)}, u32[]{:S(2)}) collective-permute-start(f32[2,16,256]{2,1,0:T(8,128)S(1)} %add.53.sum0), channel_id=1, source_target_pairs={{0,129},{1,128},{2,131},{3,130},{4,133},{5,132},{6,135},{7,134},{8... | collective-permute-start | bytes 98312 | tf_op jit(solution)/shard_map/ppermute | solution.py:72
  42.5 4.3 %collective-permute-start.11 = (f32[2,16,256]{2,1,0:T(8,128)S(1)}, f32[2,16,256]{2,1,0:T(8,128)S(1)}, u32[]{:S(2)}, u32[]{:S(2)}) collective-permute-start(f32[2,16,256]{2,1,0:T(8,128)S(1)} %add.53.sum0), channel_id=1, source_target_pairs={{0,1},{1,0},{2,3},{3,2},{4,5},{5,4},{6,7},{7,6},{8,9},{9,8},{10,11... | collective-permute-start | bytes 98312 | tf_op jit(solution)/shard_map/ppermute | solution.py:79
  42.9 3.9 %collective-permute-start.10 = (f32[2,16,256]{2,1,0:T(8,128)S(1)}, f32[2,16,256]{2,1,0:T(8,128)S(1)}, u32[]{:S(2)}, u32[]{:S(2)}) collective-permute-start(f32[2,16,256]{2,1,0:T(8,128)S(1)} %add.53.sum0), channel_id=1, source_target_pairs={{128,0},{130,2},{132,4},{134,6},{136,8},{138,10},{140,12},{142,14}... | collective-permute-start | bytes 98312 | tf_op jit(solution)/shard_map/ppermute | solution.py:44
  46.8 1.2 %copy-start = (f32[32,2,16,256]{3,2,1,0:T(8,128)S(1)}, f32[32,2,16,256]{3,2,1,0:T(8,128)}, u32[]{:S(2)}) copy-start(f32[32,2,16,256]{3,2,1,0:T(8,128)} %raw.1) | copy-start | bytes 3145732
  48.0 1.0 %copy-start.1 = (bf16[2,512,256]{2,1,0:T(8,128)(2,1)S(1)}, bf16[2,512,256]{2,1,0:T(8,128)(2,1)}, u32[]{:S(2)}) copy-start(bf16[2,512,256]{2,1,0:T(8,128)(2,1)} %constant.48.clone.all_tables) | copy-start | bytes 1572868
  49.1 0.7 copy-start.2
  58.7 13.5 %collective-permute-start.15 = (f32[16,32,128]{2,1,0:T(8,128)S(1)}, f32[16,32,128]{2,1,0:T(8,128)S(1)}, u32[]{:S(2)}, u32[]{:S(2)}) collective-permute-start(f32[16,32,128]{2,1,0:T(8,128)S(1)} %get-tuple-element.35), channel_id=1, source_target_pairs={{0,3},{1,4},{2,11},{3,18},{4,13},{5,20},{6,5},{7,2},{8,1},{9,24},{... | collective-permute-start | bytes 786440 | tf_op jit(solution)/shard_map/ppermute | solution.py:332
  72.1 9.7 %collective-permute-start.14 = (f32[16,32,128]{2,1,0:T(8,128)S(1)}, f32[16,32,128]{2,1,0:T(8,128)S(1)}, u32[]{:S(2)}, u32[]{:S(2)}) collective-permute-start(f32[16,32,128]{2,1,0:T(8,128)S(1)} %get-tuple-element.34), channel_id=1, source_target_pairs={{0,1},{1,0},{2,3},{3,2},{4,5},{5,4},{6,7},{7,6},{8,9},{9,8},{10,11... | collective-permute-start | bytes 786440 | tf_op jit(solution)/shard_map/ppermute | solution.py:79
  72.2 9.6 %collective-permute-start.16 = (f32[16,32,128]{2,1,0:T(8,128)S(1)}, f32[16,32,128]{2,1,0:T(8,128)S(1)}, u32[]{:S(2)}, u32[]{:S(2)}) collective-permute-start(f32[16,32,128]{2,1,0:T(8,128)S(1)} %get-tuple-element.37), channel_id=1, source_target_pairs={{0,2},{1,5},{2,10},{3,19},{4,12},{5,21},{6,4},{7,3},{8,0},{9,25},{... | collective-permute-start | bytes 786440 | tf_op jit(solution)/shard_map/ppermute | solution.py:332
